TPU v7x, 128 devices: a whole 4x4x4 slice. The times are simulated.
128 devices in a mesh: gx: 4 (over y), gy: 32 (over x, z, core).
Axes of the slice: x: 4, y: 4, z: 4, core: 2. Of those that a mesh axis runs over, the one named last changes fastest.
Arguments:
- populations: float32 [512, 19, 32, 1024], P(('gx', 'gy')), may hold values from 0.5 to 1.5
- solid_share: float32 [512, 32, 1024], P(('gx', 'gy')), may hold values from 0 to 0.8
- migration: int32 [512], P(('gx', 'gy')), may hold values from 0 to 511, as said below
- neighbours: int32 [512, 8], P(('gx', 'gy')), may hold values from 0 to 511, as said below
Outputs:
- passed: float32 [512, 19, 32, 1024], P(('gx', 'gy'))
Inputs may be any that keep to these rules, and one draw needn't show every extreme that they name: `migration`: A permutation of the slots; slot s lies on device s // 4 of the flattened gx+gy index. A block keeps its slot or moves into the freed slot of the device whose index differs in the lowest bit; each device hands over at most one block and receives exactly as many as it hands over. `neighbours`: the blocks form a strip of 4 columns and as many rows as devices, periodic both ways; the blocks of rows 2k and 2k+1 occupy the slots of devices 2k and 2k+1 in any order, before and after migration. So every listed neighbour slot, and the device that held that block before migration, lie on the row's own pair of devices or a pair beside it, within 3 devices along the flattened gx+gy index counted cyclically; the distance 3 occurs.
All inputs are finite; a program needn't handle non-finite values.
Results may differ from a plain program's by a relative error of at most 0.0003.
Values sent between devices are 32-bit elements; how exact they have to be, the bound alone decides.
No kernel may reach another device: no remote copies, remote signals or barrier semaphores. Data moves between devices by JAX's collectives and lax.ppermute only.
A program may use at most 192 MiB of HBM per device.

v0:
```python
import jax
import jax.numpy as jnp
from jax import lax
from jax.experimental import pallas as pl
from jax.experimental.pallas import tpu as pltpu
from jax.sharding import PartitionSpec as P

VELOCITY = [
    (0, 0, 0), (1, 0, 0), (-1, 0, 0), (0, 1, 0), (0, -1, 0), (0, 0, 1), (0, 0, -1),
    (1, 1, 0), (-1, -1, 0), (1, -1, 0), (-1, 1, 0), (1, 0, 1), (-1, 0, -1), (1, 0, -1),
    (-1, 0, 1), (0, 1, 1), (0, -1, -1), (0, 1, -1), (0, -1, 1),
]
XP = [1, 7, 9, 11, 13]
XM = [2, 10, 8, 14, 12]
YU = [3, 7, 10, 15, 17]
YD = [4, 8, 9, 16, 18]
RANGES = [(3, 2), (7, 4), (15, 4)]
F32 = jnp.float32
ANY = pl.BlockSpec(memory_space=pl.ANY)
SMEM = pl.BlockSpec(memory_space=pltpu.SMEM)
FX_AT, FY_AT, TAG_AT, MATE_TILES = 76, 81, 86, 87


def collide(f, share):
    q = 1.0 - share
    s = [None] * 19
    d = [None] * 19
    for i in range(1, 19, 2):
        s[i] = f[i] + f[i + 1]
        d[i] = f[i] - f[i + 1]
    dxy, exy = s[7] + s[9], s[7] - s[9]
    dxz, exz = s[11] + s[13], s[11] - s[13]
    dyz, eyz = s[15] + s[17], s[15] - s[17]
    sx = (s[1] + s[3]) + s[5]
    sd = (dxy + dxz) + dyz
    rho = (f[0] + sx) + sd
    axy, bxy = d[7] + d[9], d[7] - d[9]
    axz, bxz = d[11] + d[13], d[11] - d[13]
    ayz, byz = d[15] + d[17], d[15] - d[17]
    tx, ty, tz = axy + axz, bxy + ayz, bxz + byz
    jx, jy, jz = d[1] + tx, d[3] + ty, d[5] + tz
    r = pl.reciprocal(rho, approx=True)
    r = r * (2.0 - rho * r)
    vx, vy, vz = jx * r, jy * r, jz * r
    ux, uy, uz = jx * vx, jy * vy, jz * vz
    j2 = (ux + uy) + uz
    iso_a = (-173.0 / 1800.0) * f[0] + (-4.0 / 45.0) * sx + ((-29.0 / 600.0) * sd + (197.0 / 1800.0) * j2)
    iso_d = (-23.0 / 900.0) * f[0] + (-1.0 / 36.0) * sx + ((-19.0 / 300.0) * sd + (-103.0 / 900.0) * j2)
    iso_0 = (53.0 / 60.0) * f[0] + (-7.0 / 15.0) * sx + ((-5.0 / 12.0) * sd + 0.65 * j2)

    def axis_even(x, dd, u):
        return q * ((11.0 / 15.0) * x + (-1.0 / 30.0) * dd + ((-23.0 / 60.0) * u + iso_a))

    def plane_even(x, dd, u):
        return q * ((-1.0 / 30.0) * x + (23.0 / 60.0) * dd + ((5.0 / 24.0) * u + iso_d))

    q4 = 0.4 * q
    q2 = 0.2 * q
    qm = 0.2475 * q
    ex, ey, ez = axis_even(s[1], dyz, ux), axis_even(s[3], dxz, uy), axis_even(s[5], dxy, uz)
    pyz, pxz, pxy = plane_even(s[1], dyz, ux), plane_even(s[3], dxz, uy), plane_even(s[5], dxy, uz)
    hxy, hxz, hyz = q4 * (exy - jx * vy), q4 * (exz - jx * vz), q4 * (eyz - jy * vz)
    hx = q2 * ((d[1] + d[1]) - tx)
    hy = q2 * ((d[3] + d[3]) - ty)
    hz = q2 * ((d[5] + d[5]) - tz)
    gx, gy, gz = 0.25 * hx, 0.25 * hy, 0.25 * hz
    mx, my, mz = qm * (axy - axz), qm * (ayz - bxy), qm * (bxz - byz)
    axy_o, bxy_o = mx - gx, -(my + gy)
    axz_o, bxz_o = -(mx + gx), mz - gz
    ayz_o, byz_o = my - gy, -(mz + gz)
    odd = {
        1: hx, 3: hy, 5: hz,
        7: axy_o + bxy_o, 9: axy_o - bxy_o,
        11: axz_o + bxz_o, 13: axz_o - bxz_o,
        15: ayz_o + byz_o, 17: ayz_o - byz_o,
    }
    even = {
        1: ex, 3: ey, 5: ez,
        7: pxy + hxy, 9: pxy - hxy,
        11: pxz + hxz, 13: pxz - hxz,
        15: pyz + hyz, 17: pyz - hyz,
    }
    post = [None] * 19
    post[0] = f[0] - q * iso_0
    for i in range(1, 19, 2):
        w = odd[i] + share * d[i]
        post[i] = (f[i] - even[i]) - w
        post[i + 1] = (f[i + 1] - even[i]) + w
    return post


def lane_masks():
    lane = lax.broadcasted_iota(jnp.int32, (8, 128), 1)
    depth = lane & 31
    return lane, depth == 0, depth == 31


def turn(x, step_y, step_z, first, last):
    if step_z == 0:
        return x if step_y == 0 else pltpu.roll(x, (32 * step_y) % 128, 1)
    flat = 32 * step_y + step_z
    wrap = flat - 32 * step_z
    edge = first if step_z == 1 else last
    return jnp.where(edge, pltpu.roll(x, wrap % 128, 1), pltpu.roll(x, flat % 128, 1))


def unit(source, result, column, masks):
    lane, first, last = masks
    for part in range(4):
        rows = pl.ds(8 * part, 8)
        post = collide([source[c, rows, :] for c in range(19)], source[19, rows, :])
        for c in range(19):
            step_x, step_y, step_z = VELOCITY[c]
            value = turn(post[c], step_y, step_z, first, last)
            to = pl.ds(8 + 8 * part + step_x, 8)
            if step_y == 0:
                result[c, column + 1, to, :] = value
            else:
                out = (lane < 32) if step_y == 1 else (lane >= 96)
                pltpu.store(result.at[c, column + 1, to, :], value, mask=jnp.logical_not(out))
                pltpu.store(result.at[c, column + 1 + step_y, to, :], value, mask=out)


def device_index():
    return lax.axis_index("gx") * lax.axis_size("gy") + lax.axis_index("gy")


def leaver_of(migration):
    base = device_index() * 4
    leaver = jnp.int32(0)
    moving = jnp.bool_(False)
    for b in (3, 2, 1, 0):
        away = migration[b] != base + b
        leaver = jnp.where(away, b, leaver)
        moving = jnp.logical_or(moving, away)
    return leaver, moving


def column_copy(pop, share, block, column, dest, sem_p, sem_s):
    lanes = pl.ds(pl.multiple_of(column * 128, 128), 128)
    return (
        pltpu.make_async_copy(pop.at[block, :, :, lanes], dest.at[pl.ds(0, 19)], sem_p),
        pltpu.make_async_copy(share.at[block, :, lanes], dest.at[19], sem_s),
    )


def first_kernel(migration, pop, share, mate, rise, fall,
                 units, streamed, sides, rows, face, rise_v, fall_v,
                 unit_p, unit_s, side_p, side_s, row_p, row_s, out_sem, face_sem):
    masks = lane_masks()
    lane, first, last = masks
    leaver, _ = leaver_of(migration)

    def side_copies(b, high):
        return column_copy(pop, share, b, 7 * high, sides.at[high, b], side_p.at[high, b], side_s.at[high, b])

    def row_copies(b, low):
        at = pl.ds(0 if low else 31, 1)
        to = pl.ds(4 * low + b, 1)
        return (
            pltpu.make_async_copy(pop.at[b, :, at, :], rows.at[pl.ds(0, 19), to, :], row_p.at[low, b]),
            pltpu.make_async_copy(share.at[b, at, :], rows.at[19, to, :], row_s.at[low, b]),
        )

    def unit_copies(v):
        return column_copy(pop, share, leaver, v, units.at[v], unit_p.at[v], unit_s.at[v])

    for b in range(4):
        for side in range(2):
            for cp in side_copies(b, side):
                cp.start()
    for b in range(4):
        for side in range(2):
            for cp in row_copies(b, side):
                cp.start()

    def begin(v, carry):
        for cp in unit_copies(v):
            cp.start()
        return carry

    lax.fori_loop(0, 8, begin, 0)

    segment = lane // 32
    tag = jnp.zeros((8, 128), F32)
    for b in range(4):
        tag = jnp.where(segment == b, jnp.full((8, 128), migration[b], jnp.int32).astype(F32), tag)
    for v in range(8):
        face[10, :, pl.ds(128 * v, 128)] = tag
    for v in range(4):
        rise_v[5, :, pl.ds(128 * v, 128)] = tag
        fall_v[5, :, pl.ds(128 * v, 128)] = tag

    for high in (0, 1):
        for b in range(4):
            for cp in side_copies(b, high):
                cp.wait()
        comps = YU if high else YD
        for part in range(4):
            at = pl.ds(8 * part, 8)

            def packed(c):
                got = None
                for b in range(4):
                    shift = (32 * (b - 3)) % 128 if high else 32 * b
                    x = sides[high, b, c, at, :]
                    x = pltpu.roll(x, shift, 1) if shift else x
                    got = x if got is None else jnp.where(segment == b, x, got)
                return got

            post = collide([packed(c) for c in range(19)], packed(19))
            for i, c in enumerate(comps):
                value = turn(post[c], 0, VELOCITY[c][2], first, last)
                face[5 + i, :, pl.ds(128 * (part + 4 * (1 - high)), 128)] = value
                (rise_v if high else fall_v)[i, :, pl.ds(128 * part, 128)] = value

    for b in range(4):
        for side in range(2):
            for cp in row_copies(b, side):
                cp.wait()
    upper = lax.broadcasted_iota(jnp.int32, (8, 128), 0) < 4
    for v in range(8):
        at = pl.ds(128 * v, 128)
        post = collide([rows[c, :, at] for c in range(19)], rows[19, :, at])
        for i in range(5):
            value = jnp.where(upper, post[XP[i]], post[XM[i]])
            _, step_y, step_z = VELOCITY[XP[i]]
            value = turn(value, step_y, step_z, first, last)
            if step_y == 0:
                face[i, :, at] = value
            else:
                out = (lane < 32) if step_y == 1 else (lane >= 96)
                pltpu.store(face.at[i, :, at], value, mask=jnp.logical_not(out))
                beside = (v + step_y) % 8
                pltpu.store(face.at[i, :, pl.ds(128 * beside, 128)], value, mask=out)

    ends = [
        pltpu.make_async_copy(face, mate.at[pl.ds(FX_AT, 11)], face_sem.at[0]),
        pltpu.make_async_copy(rise_v, rise, face_sem.at[1]),
        pltpu.make_async_copy(fall_v, fall, face_sem.at[2]),
    ]
    for cp in ends:
        cp.start()

    def send(v):
        lanes = pl.ds(pl.multiple_of(v * 128, 128), 128)
        return [
            pltpu.make_async_copy(
                streamed.at[:, v + 1, pl.ds(8 + 8 * part, 8), :],
                mate.at[pl.ds(19 * part, 19), :, lanes],
                out_sem.at[v, part],
            )
            for part in range(4)
        ]

    def body(v, carry):
        for cp in unit_copies(v):
            cp.wait()
        unit(units.at[v], streamed, v, masks)

        @pl.when(v > 0)
        def _():
            for cp in send(v - 1):
                cp.start()

        return carry

    lax.fori_loop(0, 8, body, 0)
    for cp in send(7):
        cp.start()

    def finish(v, carry):
        for cp in send(v):
            cp.wait()
        return carry

    lax.fori_loop(0, 8, finish, 0)
    for cp in ends:
        cp.wait()


def second_kernel(migration, pop, share, after, out, units, streamed, unit_p, unit_s, out_sem):
    masks = lane_masks()
    leaver, _ = leaver_of(migration)

    def block(j):
        return j + (j >= leaver).astype(jnp.int32)

    def copies(u):
        return column_copy(pop, share, block(u // 8), u % 8, units.at[u], unit_p.at[u], unit_s.at[u])

    def send(u):
        lanes = pl.ds(pl.multiple_of((u % 8) * 128, 128), 128)
        return pltpu.make_async_copy(
            streamed.at[u // 8, :, u % 8 + 1, pl.ds(8, 32), :],
            out.at[block(u // 8), :, :, lanes],
            out_sem.at[u],
        )

    def begin(u, carry):
        for cp in copies(u):
            cp.start()
        return carry

    lax.fori_loop(0, 24, begin, 0)

    def body(u, carry):
        for cp in copies(u):
            cp.wait()
        unit(units.at[u], streamed.at[u // 8], u % 8, masks)

        @pl.when(u % 8 > 0)
        def _():
            send(u - 1).start()

        @pl.when(u % 8 == 7)
        def _():
            send(u).start()

        return carry

    lax.fori_loop(0, 24, body, 0)

    def finish(u, carry):
        send(u).wait()
        return carry

    lax.fori_loop(0, 24, finish, 0)


def third_kernel(neighbours, migration, mine, got, low_a, low_b, high_a, high_b, out_in, out,
                 filled, sides, fx, fy, tags, table,
                 fill_sem, side_sem, face_sem, tag_sem, row_sem):
    del out_in
    base = device_index() * 4
    pair = base // 8 * 8
    leaver, moving = leaver_of(migration)
    lane = lax.broadcasted_iota(jnp.int32, (8, 128), 1)
    sub = lax.broadcasted_iota(jnp.int32, (8, 128), 0)

    def block(j):
        return j + (j >= leaver).astype(jnp.int32)

    def fills(source):
        return [
            pltpu.make_async_copy(source.at[pl.ds(19 * part, 19)], filled.at[part], fill_sem.at[part])
            for part in range(4)
        ]

    tag_copies = [pltpu.make_async_copy(got.at[TAG_AT, pl.ds(0, 1), pl.ds(0, 128)], tags.at[pl.ds(0, 1)], tag_sem.at[0])]
    for k, ref in enumerate((low_a, low_b, high_a, high_b)):
        tag_copies.append(
            pltpu.make_async_copy(ref.at[5, pl.ds(0, 1), pl.ds(0, 128)], tags.at[pl.ds(k + 1, 1)], tag_sem.at[k + 1])
        )
    face_copies = [
        pltpu.make_async_copy(mine.at[pl.ds(FX_AT, 5)], fx.at[0], face_sem.at[0]),
        pltpu.make_async_copy(got.at[pl.ds(FX_AT, 5)], fx.at[1], face_sem.at[1]),
        pltpu.make_async_copy(mine.at[pl.ds(FY_AT, 5)], fy.at[0], face_sem.at[2]),
        pltpu.make_async_copy(got.at[pl.ds(FY_AT, 5)], fy.at[1], face_sem.at[3]),
    ]
    for k, ref in enumerate((low_a, low_b, high_a, high_b)):
        lanes = pl.ds(0 if k < 2 else 512, 512)
        face_copies.append(
            pltpu.make_async_copy(ref.at[pl.ds(0, 5)], fy.at[k + 2, :, :, lanes], face_sem.at[k + 4])
        )
    for cp in tag_copies + face_copies:
        cp.start()

    @pl.when(moving)
    def _():
        for cp in fills(got):
            cp.start()

    @pl.when(jnp.logical_not(moving))
    def _():
        for cp in fills(mine):
            cp.start()

    def side_copies(j, back):
        made = []
        for high in range(2):
            at = 0
            for k, (start, size) in enumerate(RANGES):
                there = out.at[block(j), pl.ds(start, size), :, pl.ds(896 * high, 128)]
                here = sides.at[j, high, pl.ds(at, size)]
                sem = side_sem.at[j, high, k]
                made.append(pltpu.make_async_copy(here, there, sem) if back else pltpu.make_async_copy(there, here, sem))
                at += size
        return made

    for j in range(3):
        for cp in side_copies(j, False):
            cp.start()

    for cp in tag_copies:
        cp.wait()
    for b in range(4):
        table[migration[b] & 7] = b
        table[tags[0, 32 * b].astype(jnp.int32) & 7] = 4 + b
        for k in range(4):
            table[(8 if k < 2 else 16) + (tags[k + 1, 32 * b].astype(jnp.int32) & 7)] = 4 * (k + 2) + b

    def find(b, k, beside):
        slot = neighbours[b, k]
        code = table[(slot & 7) + jnp.where(slot // 8 * 8 == pair, 0, beside)]
        return code // 4, code % 4

    for cp in face_copies:
        cp.wait()

    def with_row(now, where, step_x, k, column):
        src, j = where
        home, start = (0, 0) if step_x == 1 else (7, 4)
        row = pltpu.roll(fx[src, k, :, pl.ds(128 * column, 128)], (home + 8 - start - j) % 8, 0)
        return jnp.where(sub == home, row, now)

    def patch(b, read, write):
        xs = {1: find(b, 1, 0), -1: find(b, 0, 0)}
        corners = {
            (1, 1): find(b, 5, 8), (-1, 1): find(b, 6, 8),
            (-1, -1): find(b, 4, 16), (1, -1): find(b, 7, 16),
        }
        for high in (0, 1):
            flow = -1 if high else 1
            comps = YD if high else YU
            home = 3 if high else 0
            source, at = find(b, 2 if high else 3, 16 if high else 8)

            def tile(where, i, part):
                src, j = where
                x = fy[src, i, :, pl.ds(128 * (part + 4 * high), 128)]
                return pltpu.roll(x, (32 * (home + 4 - j)) % 128, 1)

            edge = (lane >= 96) if high else (lane < 32)
            for c in (3, 4, 7, 8, 9, 10, 15, 16, 17, 18):
                step_x, step_y, _ = VELOCITY[c]
                in_y = step_y == flow
                if not in_y and step_x == 0:
                    continue
                if in_y:
                    i = comps.index(c)
                    tiles = [tile((source, at), i, part) for part in range(4)]
                    if step_x == 1:
                        near = [tile(corners[(1, step_y)], i, 3)] + tiles
                        near = [pltpu.roll(t, 1, 0) for t in near]
                        tiles = [jnp.where(sub == 0, near[p], near[p + 1]) for p in range(4)]
                    elif step_x == -1:
                        near = tiles + [tile(corners[(-1, step_y)], i, 0)]
                        near = [pltpu.roll(t, 7, 0) for t in near]
                        tiles = [jnp.where(sub == 7, near[p + 1], near[p]) for p in range(4)]
                for part in range(4):
                    in_x = (step_x == 1 and part == 0) or (step_x == -1 and part == 3)
                    if not in_y and not in_x:
                        continue
                    now = read(c, part, high)
                    if in_x:
                        k = (XP if step_x == 1 else XM).index(c)
                        now = with_row(now, xs[step_x], step_x, k, 7 * high)
                    if in_y:
                        now = jnp.where(edge, tiles[part], now)
                    write(c, part, high, now)
        return xs

    order = (3, 4, 7, 8, 9, 10, 15, 16, 17, 18)

    def row_copies(j, xs):
        made = []
        for step_x, comps in ((1, XP), (-1, XM)):
            src, at = xs[step_x]
            for k, c in enumerate(comps):
                lanes = pl.ds(0, 1024) if VELOCITY[c][1] == 0 else pl.ds(128, 768)
                made.append(
                    pltpu.make_async_copy(
                        fx.at[src, k, pl.ds(at + (0 if step_x == 1 else 4), 1), lanes],
                        out.at[block(j), c, pl.ds(0 if step_x == 1 else 31, 1), lanes],
                        row_sem.at[j, k + (0 if step_x == 1 else 5)],
                    )
                )
        return made

    pending = []
    for j in range(3):
        b = block(j)
        for cp in side_copies(j, False):
            cp.wait()

        def read(c, part, high, j=j):
            return sides[j, high, order.index(c), pl.ds(8 * part, 8), :]

        def write(c, part, high, value, j=j):
            sides[j, high, order.index(c), pl.ds(8 * part, 8), :] = value

        xs = patch(b, read, write)
        made = row_copies(j, xs) + side_copies(j, True)
        for cp in made:
            cp.start()
        pending += made

    for cp in fills(got):
        cp.wait()

    def read_filled(c, part, high):
        return filled[part, c, :, pl.ds(896 * high, 128)]

    def write_filled(c, part, high, value):
        filled[part, c, :, pl.ds(896 * high, 128)] = value

    xs = patch(leaver, read_filled, write_filled)
    for step_x, comps in ((1, XP), (-1, XM)):
        part = 0 if step_x == 1 else 3
        for k, c in enumerate(comps):
            for column in range(8) if VELOCITY[c][1] == 0 else range(1, 7):
                lanes = pl.ds(128 * column, 128)
                filled[part, c, :, lanes] = with_row(filled[part, c, :, lanes], xs[step_x], step_x, k, column)
    for part in range(4):
        cp = pltpu.make_async_copy(filled.at[part], out.at[leaver, :, pl.ds(8 * part, 8), :], fill_sem.at[part])
        cp.start()
        pending.append(cp)
    for cp in pending:
        cp.wait()


def route(shift, cross):
    count = lax.axis_size("gx") * lax.axis_size("gy")
    return [(d, ((d + shift) % count) ^ cross) for d in range(count)]


def on_device(populations, solid_share, migration, neighbours):
    limit = 56 * 2**20
    dma = pltpu.SemaphoreType.DMA
    mate, rise, fall = pl.pallas_call(
        first_kernel,
        name="faces_and_leaver",
        out_shape=(
            jax.ShapeDtypeStruct((MATE_TILES, 8, 1024), F32),
            jax.ShapeDtypeStruct((6, 8, 512), F32),
            jax.ShapeDtypeStruct((6, 8, 512), F32),
        ),
        in_specs=[SMEM, ANY, ANY],
        out_specs=(ANY, ANY, ANY),
        scratch_shapes=[
            pltpu.VMEM((8, 20, 32, 128), F32),
            pltpu.VMEM((19, 10, 48, 128), F32),
            pltpu.VMEM((2, 4, 20, 32, 128), F32),
            pltpu.VMEM((20, 8, 1024), F32),
            pltpu.VMEM((11, 8, 1024), F32),
            pltpu.VMEM((6, 8, 512), F32),
            pltpu.VMEM((6, 8, 512), F32),
            dma((8,)), dma((8,)), dma((2, 4)), dma((2, 4)), dma((2, 4)), dma((2, 4)), dma((8, 4)), dma((3,)),
        ],
        compiler_params=pltpu.CompilerParams(vmem_limit_bytes=limit),
        cost_estimate=pl.CostEstimate(flops=20_000_000, bytes_accessed=9_000_000, transcendentals=0),
    )(migration, populations, solid_share)

    axes = ("gx", "gy")
    got = lax.ppermute(mate, axes, route(0, 1))
    low_a = lax.ppermute(rise, axes, route(2, 0))
    high_a = lax.ppermute(fall, axes, route(-2, 0))
    low_b = lax.ppermute(rise, axes, route(2, 1))
    high_b = lax.ppermute(fall, axes, route(-2, 1))

    out = pl.pallas_call(
        second_kernel,
        name="staying_blocks",
        out_shape=jax.ShapeDtypeStruct((4, 19, 32, 1024), F32),
        in_specs=[SMEM, ANY, ANY, ANY],
        out_specs=ANY,
        scratch_shapes=[
            pltpu.VMEM((24, 20, 32, 128), F32),
            pltpu.VMEM((3, 19, 10, 48, 128), F32),
            dma((24,)), dma((24,)), dma((24,)),
        ],
        compiler_params=pltpu.CompilerParams(vmem_limit_bytes=limit),
        cost_estimate=pl.CostEstimate(flops=30_000_000, bytes_accessed=16_000_000, transcendentals=0),
    )(migration, populations, solid_share, rise)

    return pl.pallas_call(
        third_kernel,
        name="patch_boundaries",
        out_shape=jax.ShapeDtypeStruct((4, 19, 32, 1024), F32),
        in_specs=[SMEM, SMEM] + [ANY] * 7,
        out_specs=ANY,
        input_output_aliases={8: 0},
        scratch_shapes=[
            pltpu.VMEM((4, 19, 8, 1024), F32),
            pltpu.VMEM((3, 2, 10, 32, 128), F32),
            pltpu.VMEM((2, 5, 8, 1024), F32),
            pltpu.VMEM((6, 5, 8, 1024), F32),
            pltpu.SMEM((5, 128), F32),
            pltpu.SMEM((24,), jnp.int32),
            dma((4,)), dma((3, 2, 3)), dma((8,)), dma((5,)), dma((3, 10)),
        ],
        compiler_params=pltpu.CompilerParams(vmem_limit_bytes=limit),
        cost_estimate=pl.CostEstimate(flops=1_000_000, bytes_accessed=8_000_000, transcendentals=0),
    )(neighbours, migration, mate, got, low_a, low_b, high_a, high_b, out)


def solution(mesh):
    return jax.shard_map(
        on_device,
        mesh=mesh,
        in_specs=(
            P(("gx", "gy"), None, None, None),
            P(("gx", "gy"), None, None),
            P(("gx", "gy")),
            P(("gx", "gy"), None),
        ),
        out_specs=P(("gx", "gy"), None, None, None),
        check_vma=False,
    )
```

profile of v0, /device:TPU:1, one launch (start us, length us, event | category | flops | bytes accessed | tf_op | source)
XLA Modules:
  0.0 38.4 jit_solution(16361908868416472990)
XLA Ops:
  0.0 7.2 %faces_and_leaver.1 = (f32[87,8,1024]{2,1,0:T(8,128)}, f32[6,8,512]{2,1,0:T(8,128)}, f32[6,8,512]{2,1,0:T(8,128)}) custom-call(s32[4]{0:T(128)} %migration.5, f32[4,19,32,1024]{3,2,1,0:T(8,128)} %pop.3, f32[4,32,1024]{2,1,0:T(8,128)} %share.3), custom_call_target="tpu_custom_call" | custom-call | flops 20000000 | bytes 9000000 | tf_op jit(solution)/shard_map/faces_and_leaver/pallas_call | solution.py:531
  7.2 1.5 %collective-permute-start = (f32[87,8,1024]{2,1,0:T(8,128)}, f32[87,8,1024]{2,1,0:T(8,128)S(1)}, u32[]{:S(2)}, u32[]{:S(2)}) collective-permute-start(f32[87,8,1024]{2,1,0:T(8,128)} %get-tuple-element.8.mine), channel_id=1, source_target_pairs={{0,1},{1,0},{2,3},{3,2},{4,5},{5,4},{6,7},{7,6},{8,9},{9,8},{10,11... | collective-permute-start | bytes 8552456 | tf_op jit(solution)/shard_map/ppermute | solution.py:556
  8.7 8.5 %collective-permute-start.4 = (f32[6,8,512]{2,1,0:T(8,128)}, f32[6,8,512]{2,1,0:T(8,128)S(1)}, u32[]{:S(2)}, u32[]{:S(2)}) collective-permute-start(f32[6,8,512]{2,1,0:T(8,128)} %get-tuple-element.10), channel_id=1, source_target_pairs={{0,127},{1,126},{2,1},{3,0},{4,3},{5,2},{6,5},{7,4},{8,7},{9,6},{1... | collective-permute-start | bytes 294920 | tf_op jit(solution)/shard_map/ppermute | solution.py:560
  17.1 0.1 collective-permute-start.3
  17.2 2.0 %collective-permute-start.2 = (f32[6,8,512]{2,1,0:T(8,128)}, f32[6,8,512]{2,1,0:T(8,128)S(1)}, u32[]{:S(2)}, u32[]{:S(2)}) collective-permute-start(f32[6,8,512]{2,1,0:T(8,128)} %get-tuple-element.9.after), channel_id=1, source_target_pairs={{0,3},{1,2},{2,5},{3,4},{4,7},{5,6},{6,9},{7,8},{8,11},{9,10},{10,... | collective-permute-start | bytes 294920 | tf_op jit(solution)/shard_map/ppermute | solution.py:559
  19.2 0.0 collective-permute-start.1
  19.2 9.2 %staying_blocks.1.out_in = f32[4,19,32,1024]{3,2,1,0:T(8,128)} custom-call(s32[4]{0:T(128)} %migration.5, f32[4,19,32,1024]{3,2,1,0:T(8,128)} %pop.3, f32[4,32,1024]{2,1,0:T(8,128)} %share.3, f32[6,8,512]{2,1,0:T(8,128)} %get-tuple-element.9.after), custom_call_target="tpu_custom_call" | custom-call | flops 30000000 | bytes 16000000 | tf_op jit(solution)/shard_map/staying_blocks/pallas_call | solution.py:562
  28.4 0.0 collective-permute-done.4.high_b
  28.4 0.0 copy-start.1
  28.4 0.0 collective-permute-done.3.high_a
  28.5 0.0 copy-start.2
  28.5 0.0 collective-permute-done.2.low_b
  28.5 0.0 copy-start.3
  28.5 1.9 %collective-permute-done.1.low_a = f32[6,8,512]{2,1,0:T(8,128)S(1)} collective-permute-done((f32[6,8,512]{2,1,0:T(8,128)}, f32[6,8,512]{2,1,0:T(8,128)S(1)}, u32[]{:S(2)}, u32[]{:S(2)}) %collective-permute-start.1) | collective-permute-done | bytes 98336 | tf_op jit(solution)/shard_map/ppermute | solution.py:557
  30.4 0.0 copy-start.4
  30.4 0.0 collective-permute-done.got
  30.4 0.0 copy-done.1
  30.4 0.0 copy-done.2
  30.4 0.0 copy-done.3
  30.4 0.6 %copy-done.4 = f32[6,8,512]{2,1,0:T(8,128)} copy-done((f32[6,8,512]{2,1,0:T(8,128)}, f32[6,8,512]{2,1,0:T(8,128)S(1)}, u32[]{:S(2)}) %copy-start.4) | copy-done | bytes 98328
  31.0 0.0 copy-start
  31.0 1.6 %copy-done = f32[87,8,1024]{2,1,0:T(8,128)} copy-done((f32[87,8,1024]{2,1,0:T(8,128)}, f32[87,8,1024]{2,1,0:T(8,128)S(1)}, u32[]{:S(2)}) %copy-start) | copy-done | bytes 2850840
  32.6 5.8 %patch_boundaries.1 = f32[4,19,32,1024]{3,2,1,0:T(8,128)} custom-call(s32[4,8]{1,0:T(4,128)} %neighbours.1, s32[4]{0:T(128)} %migration.5, f32[87,8,1024]{2,1,0:T(8,128)} %get-tuple-element.8.mine, f32[87,8,1024]{2,1,0:T(8,128)} %copy-done, f32[6,8,512]{2,1,0:T(8,128)} %copy-done.4, f32[6,8,512]{2,1,0:T(8,128)} %copy-done.3, ...), custom_call_target="tpu_custom_call", output_to_operand_aliasing={{}: (8, {})} | custom-call | flops 1000000 | bytes 8000000 | tf_op jit(solution)/shard_map/patch_boundaries/pallas_call | solution.py:577
Async XLA Ops:
  7.2 23.2 %collective-permute-start = (f32[87,8,1024]{2,1,0:T(8,128)}, f32[87,8,1024]{2,1,0:T(8,128)S(1)}, u32[]{:S(2)}, u32[]{:S(2)}) collective-permute-start(f32[87,8,1024]{2,1,0:T(8,128)} %get-tuple-element.8.mine), channel_id=1, source_target_pairs={{0,1},{1,0},{2,3},{3,2},{4,5},{5,4},{6,7},{7,6},{8,9},{9,8},{10,11... | collective-permute-start | bytes 8552456 | tf_op jit(solution)/shard_map/ppermute | solution.py:556
  8.7 19.8 %collective-permute-start.4 = (f32[6,8,512]{2,1,0:T(8,128)}, f32[6,8,512]{2,1,0:T(8,128)S(1)}, u32[]{:S(2)}, u32[]{:S(2)}) collective-permute-start(f32[6,8,512]{2,1,0:T(8,128)} %get-tuple-element.10), channel_id=1, source_target_pairs={{0,127},{1,126},{2,1},{3,0},{4,3},{5,2},{6,5},{7,4},{8,7},{9,6},{1... | collective-permute-start | bytes 294920 | tf_op jit(solution)/shard_map/ppermute | solution.py:560
  17.1 11.3 %collective-permute-start.3 = (f32[6,8,512]{2,1,0:T(8,128)}, f32[6,8,512]{2,1,0:T(8,128)S(1)}, u32[]{:S(2)}, u32[]{:S(2)}) collective-permute-start(f32[6,8,512]{2,1,0:T(8,128)} %get-tuple-element.10), channel_id=1, source_target_pairs={{0,126},{1,127},{2,0},{3,1},{4,2},{5,3},{6,4},{7,5},{8,6},{9,7},{1... | collective-permute-start | bytes 294920 | tf_op jit(solution)/shard_map/ppermute | solution.py:558
  17.2 11.2 %collective-permute-start.2 = (f32[6,8,512]{2,1,0:T(8,128)}, f32[6,8,512]{2,1,0:T(8,128)S(1)}, u32[]{:S(2)}, u32[]{:S(2)}) collective-permute-start(f32[6,8,512]{2,1,0:T(8,128)} %get-tuple-element.9.after), channel_id=1, source_target_pairs={{0,3},{1,2},{2,5},{3,4},{4,7},{5,6},{6,9},{7,8},{8,11},{9,10},{10,... | collective-permute-start | bytes 294920 | tf_op jit(solution)/shard_map/ppermute | solution.py:559
  19.2 11.2 %collective-permute-start.1 = (f32[6,8,512]{2,1,0:T(8,128)}, f32[6,8,512]{2,1,0:T(8,128)S(1)}, u32[]{:S(2)}, u32[]{:S(2)}) collective-permute-start(f32[6,8,512]{2,1,0:T(8,128)} %get-tuple-element.9.after), channel_id=1, source_target_pairs={{0,2},{1,3},{2,4},{3,5},{4,6},{5,7},{6,8},{7,9},{8,10},{9,11},{10,... | collective-permute-start | bytes 294920 | tf_op jit(solution)/shard_map/ppermute | solution.py:557
  28.4 1.9 %copy-start.1 = (f32[6,8,512]{2,1,0:T(8,128)}, f32[6,8,512]{2,1,0:T(8,128)S(1)}, u32[]{:S(2)}) copy-start(f32[6,8,512]{2,1,0:T(8,128)S(1)} %collective-permute-done.4.high_b) | copy-start | bytes 294916
  28.5 1.9 %copy-start.2 = (f32[6,8,512]{2,1,0:T(8,128)}, f32[6,8,512]{2,1,0:T(8,128)S(1)}, u32[]{:S(2)}) copy-start(f32[6,8,512]{2,1,0:T(8,128)S(1)} %collective-permute-done.3.high_a) | copy-start | bytes 294916
  28.5 1.9 %copy-start.3 = (f32[6,8,512]{2,1,0:T(8,128)}, f32[6,8,512]{2,1,0:T(8,128)S(1)}, u32[]{:S(2)}) copy-start(f32[6,8,512]{2,1,0:T(8,128)S(1)} %collective-permute-done.2.low_b) | copy-start | bytes 294916
  30.4 0.6 %copy-start.4 = (f32[6,8,512]{2,1,0:T(8,128)}, f32[6,8,512]{2,1,0:T(8,128)S(1)}, u32[]{:S(2)}) copy-start(f32[6,8,512]{2,1,0:T(8,128)S(1)} %collective-permute-done.1.low_a) | copy-start | bytes 294916
  31.0 1.6 %copy-start = (f32[87,8,1024]{2,1,0:T(8,128)}, f32[87,8,1024]{2,1,0:T(8,128)S(1)}, u32[]{:S(2)}) copy-start(f32[87,8,1024]{2,1,0:T(8,128)S(1)} %collective-permute-done.got) | copy-start | bytes 8552452
where the time goes:
time: 38.6 us; the launch traced here: 38.4 us
  Pallas kernels  22.2 us (58%)
  starting transfers between devices  12 us (31%)
  local copies, waits for them, and re-layouts  2.23 us (6%)
  waiting for transfers between devices  1.88 us (5%)
    pallas_call x1, Pallas kernels, on_device(): pl.pallas_call(second_kernel, name='staying_blocks', out_shape=jax.ShapeD...  9.21 us
    ppermute x1, starting transfers between devices, on_device(): high_b = lax.ppermute(fall, axes, route(-2, 1))  8.45 us
    pallas_call x1, Pallas kernels, on_device(): pl.pallas_call(first_kernel, name='faces_and_leaver', out_shape=(jax.Shap...  7.16 us
    pallas_call x1, Pallas kernels, on_device(): pl.pallas_call(third_kernel, name='patch_boundaries', out_shape=jax.Shape...  5.83 us
    unnamed x10, local copies, waits for them, and re-layouts  2.23 us
    ppermute x1, starting transfers between devices, on_device(): low_b = lax.ppermute(rise, axes, route(2, 1))  1.95 us
    ppermute x1, waiting for transfers between devices, on_device(): low_a = lax.ppermute(rise, axes, route(2, 0))  1.87 us
    ppermute x1, starting transfers between devices, on_device(): got = lax.ppermute(mate, axes, route(0, 1))  1.5 us
  transfers between devices with their start and end apart: 5, of which 1 were waited for; matrix products, arithmetic and copies ran while one was open for 0% of the time, Pallas kernels for 24%

commit v1 on v0

v1 whole, which is shorter than its diff:
```python
import jax
import jax.numpy as jnp
from jax import lax
from jax.experimental import pallas as pl
from jax.experimental.pallas import tpu as pltpu
from jax.sharding import PartitionSpec as P

VELOCITY = [
    (0, 0, 0), (1, 0, 0), (-1, 0, 0), (0, 1, 0), (0, -1, 0), (0, 0, 1), (0, 0, -1),
    (1, 1, 0), (-1, -1, 0), (1, -1, 0), (-1, 1, 0), (1, 0, 1), (-1, 0, -1), (1, 0, -1),
    (-1, 0, 1), (0, 1, 1), (0, -1, -1), (0, 1, -1), (0, -1, 1),
]
XP = [1, 7, 9, 11, 13]
XM = [2, 10, 8, 14, 12]
YU = [3, 7, 10, 15, 17]
YD = [4, 8, 9, 16, 18]
F32 = jnp.float32
LIMITS = (12, 8, 12)
HBM = pl.BlockSpec(memory_space=pltpu.HBM)
VMEM = pl.BlockSpec(memory_space=pltpu.VMEM)
SMEM = pl.BlockSpec(memory_space=pltpu.SMEM)
FX_AT, FU_AT, FD_AT, TAG_AT, MATE = 152, 162, 167, 172, 173


def collide(f, share):
    q = 1.0 - share
    s = [None] * 19
    d = [None] * 19
    for i in range(1, 19, 2):
        s[i] = f[i] + f[i + 1]
        d[i] = f[i] - f[i + 1]
    dxy, exy = s[7] + s[9], s[7] - s[9]
    dxz, exz = s[11] + s[13], s[11] - s[13]
    dyz, eyz = s[15] + s[17], s[15] - s[17]
    sx = (s[1] + s[3]) + s[5]
    sd = (dxy + dxz) + dyz
    rho = (f[0] + sx) + sd
    axy, bxy = d[7] + d[9], d[7] - d[9]
    axz, bxz = d[11] + d[13], d[11] - d[13]
    ayz, byz = d[15] + d[17], d[15] - d[17]
    tx, ty, tz = axy + axz, bxy + ayz, bxz + byz
    jx, jy, jz = d[1] + tx, d[3] + ty, d[5] + tz
    r = pl.reciprocal(rho, approx=True)
    r = r * (2.0 - rho * r)
    vx, vy, vz = jx * r, jy * r, jz * r
    ux, uy, uz = jx * vx, jy * vy, jz * vz
    j2 = (ux + uy) + uz
    iso_a = (-173.0 / 1800.0) * f[0] + (-4.0 / 45.0) * sx + ((-29.0 / 600.0) * sd + (197.0 / 1800.0) * j2)
    iso_d = (-23.0 / 900.0) * f[0] + (-1.0 / 36.0) * sx + ((-19.0 / 300.0) * sd + (-103.0 / 900.0) * j2)
    iso_0 = (53.0 / 60.0) * f[0] + (-7.0 / 15.0) * sx + ((-5.0 / 12.0) * sd + 0.65 * j2)

    def axis_even(x, dd, u):
        return q * ((11.0 / 15.0) * x + (-1.0 / 30.0) * dd + ((-23.0 / 60.0) * u + iso_a))

    def plane_even(x, dd, u):
        return q * ((-1.0 / 30.0) * x + (23.0 / 60.0) * dd + ((5.0 / 24.0) * u + iso_d))

    q4 = 0.4 * q
    q2 = 0.2 * q
    qm = 0.2475 * q
    ex, ey, ez = axis_even(s[1], dyz, ux), axis_even(s[3], dxz, uy), axis_even(s[5], dxy, uz)
    pyz, pxz, pxy = plane_even(s[1], dyz, ux), plane_even(s[3], dxz, uy), plane_even(s[5], dxy, uz)
    hxy, hxz, hyz = q4 * (exy - jx * vy), q4 * (exz - jx * vz), q4 * (eyz - jy * vz)
    hx = q2 * ((d[1] + d[1]) - tx)
    hy = q2 * ((d[3] + d[3]) - ty)
    hz = q2 * ((d[5] + d[5]) - tz)
    gx, gy, gz = 0.25 * hx, 0.25 * hy, 0.25 * hz
    mx, my, mz = qm * (axy - axz), qm * (ayz - bxy), qm * (bxz - byz)
    axy_o, bxy_o = mx - gx, -(my + gy)
    axz_o, bxz_o = -(mx + gx), mz - gz
    ayz_o, byz_o = my - gy, -(mz + gz)
    odd = {
        1: hx, 3: hy, 5: hz,
        7: axy_o + bxy_o, 9: axy_o - bxy_o,
        11: axz_o + bxz_o, 13: axz_o - bxz_o,
        15: ayz_o + byz_o, 17: ayz_o - byz_o,
    }
    even = {
        1: ex, 3: ey, 5: ez,
        7: pxy + hxy, 9: pxy - hxy,
        11: pxz + hxz, 13: pxz - hxz,
        15: pyz + hyz, 17: pyz - hyz,
    }
    post = [None] * 19
    post[0] = f[0] - q * iso_0
    for i in range(1, 19, 2):
        w = odd[i] + share * d[i]
        post[i] = (f[i] - even[i]) - w
        post[i + 1] = (f[i + 1] - even[i]) + w
    return post


def lane_tables():
    lane = lax.broadcasted_iota(jnp.int32, (8, 128), 1)
    tables = {}
    for step_y in (-1, 0, 1):
        for step_z in (-1, 1):
            tables[step_y, step_z] = ((lane - 32 * step_y) & 96) | ((lane - step_z) & 31)
    return lane, tables


def turn(x, step_y, step_z, tables):
    if step_z:
        return jnp.take_along_axis(x, tables[step_y, step_z], axis=1)
    return pltpu.roll(x, (32 * step_y) % 128, 1) if step_y else x


def unit(source, result, column, lanes_of):
    lane, tables = lanes_of
    at = pl.ds(pl.multiple_of(column * 128, 128), 128)
    for part in range(4):
        rows = pl.ds(8 * part, 8)
        post = collide([source[c, rows, at] for c in range(19)], source[19, rows, at])
        for c in range(19):
            step_x, step_y, step_z = VELOCITY[c]
            value = turn(post[c], step_y, step_z, tables)
            to = pl.ds(8 + 8 * part + step_x, 8)
            if step_y == 0:
                result[c, column + 1, to, :] = value
            else:
                out = (lane < 32) if step_y == 1 else (lane >= 96)
                pltpu.store(result.at[c, column + 1, to, :], value, mask=jnp.logical_not(out))
                pltpu.store(result.at[c, column + 1 + step_y, to, :], value, mask=out)


def device_index():
    return lax.axis_index("gx") * lax.axis_size("gy") + lax.axis_index("gy")


def leaver_of(migration):
    base = device_index() * 4
    leaver = jnp.int32(0)
    moving = jnp.bool_(False)
    for b in (3, 2, 1, 0):
        away = migration[b] != base + b
        leaver = jnp.where(away, b, leaver)
        moving = jnp.logical_or(moving, away)
    return leaver, moving


def staying(j, leaver):
    return j + (j >= leaver).astype(jnp.int32)


def early_blocks():
    return jnp.int32(1)


def first_kernel(migration, pop, share, raw, streamed, mate, rise, fall, leaving, pop_sem, share_sem, mate_sem):
    lanes_of = lane_tables()
    lane, tables = lanes_of
    leaver, _ = leaver_of(migration)

    def block(p):
        return jnp.where(p == 0, leaver, staying(p - 1, leaver))

    def load(p):
        return (
            pltpu.make_async_copy(pop.at[block(p)], raw.at[p, pl.ds(0, 19)], pop_sem.at[p]),
            pltpu.make_async_copy(share.at[block(p)], raw.at[p, 19], share_sem.at[p]),
        )

    for p in range(4):
        for cp in load(p):
            cp.start()

    segment = lane >> 5
    tag = jnp.zeros((8, 128), F32)
    for p in range(4):
        tag = jnp.where(segment == p, jnp.full((8, 128), migration[block(p)], jnp.int32).astype(F32), tag)
    mate[TAG_AT, pl.ds(0, 8), :] = tag
    rise[5, pl.ds(0, 8), :] = tag
    fall[5, pl.ds(0, 8), :] = tag

    def hand(v):
        return pltpu.make_async_copy(
            leaving.at[:, v + 1, pl.ds(8, 32), :], mate.at[pl.ds(19 * v, 19)], mate_sem.at[v]
        )

    for cp in load(0):
        cp.wait()

    def leaving_unit(v, carry):
        unit(raw.at[0], leaving, v, lanes_of)

        @pl.when(v > 0)
        def _():
            hand(v - 1).start()

        return carry

    lax.fori_loop(0, 8, leaving_unit, 0)
    hand(7).start()

    def early(j, carry):
        for cp in load(j + 1):
            cp.wait()

        def one(v, inner):
            unit(raw.at[j + 1], streamed.at[j], v, lanes_of)
            return inner

        return lax.fori_loop(0, 8, one, carry)

    lax.fori_loop(0, early_blocks(), early, 0)

    def rest(j, carry):
        for cp in load(j + 1):
            cp.wait()
        return carry

    lax.fori_loop(early_blocks(), 3, rest, 0)

    for high in (0, 1):
        column = pl.ds(896 * high, 128)
        for part in range(4):
            rows = pl.ds(8 * part, 8)

            def packed(c):
                got = None
                for p in range(4):
                    shift = (32 * (p - 3)) % 128 if high else 32 * p
                    x = raw[p, c, rows, column]
                    x = pltpu.roll(x, shift, 1) if shift else x
                    got = x if got is None else jnp.where(segment == p, x, got)
                return got

            post = collide([packed(c) for c in range(19)], packed(19))
            for i, c in enumerate(YU if high else YD):
                value = turn(post[c], 0, VELOCITY[c][2], tables)
                mate[(FU_AT if high else FD_AT) + i, rows, :] = value
                (rise if high else fall)[i, rows, :] = value

    sub = lax.broadcasted_iota(jnp.int32, (8, 128), 0)

    def x_faces(v, carry):
        column = pl.ds(pl.multiple_of(v * 128, 128), 128)

        def packed(c):
            got = None
            for p in range(4):
                x = pltpu.roll(raw[p, c, pl.ds(24, 8), column], (p + 1) % 8, 0)
                y = pltpu.roll(raw[p, c, pl.ds(0, 8), column], p + 4, 0)
                got = x if got is None else jnp.where(sub == p, x, got)
                got = jnp.where(sub == p + 4, y, got)
            return got

        post = collide([packed(c) for c in range(19)], packed(19))
        for i in range(5):
            value = jnp.where(sub < 4, post[XP[i]], post[XM[i]])
            _, step_y, step_z = VELOCITY[XP[i]]
            value = turn(value, step_y, step_z, tables)

            def place(v, k):
                return mate.at[FX_AT + 2 * i + (v >> 2), pl.ds(pl.multiple_of((v & 3) * 8, 8), 8), :]

            if step_y == 0:
                place(v, i)[...] = value
            else:
                out = (lane < 32) if step_y == 1 else (lane >= 96)
                pltpu.store(place(v, i), value, mask=jnp.logical_not(out))
                pltpu.store(place((v + step_y) & 7, i), value, mask=out)
        return carry

    lax.fori_loop(0, 8, x_faces, 0)
    for v in range(8):
        hand(v).wait()


def second_kernel(migration, raw, held, after, out, streamed, out_sem):
    del held, after
    lanes_of = lane_tables()
    leaver, _ = leaver_of(migration)

    def send(j, v):
        return pltpu.make_async_copy(
            streamed.at[j, :, v + 1, pl.ds(8, 32), :],
            out.at[staying(j, leaver), :, :, pl.ds(pl.multiple_of(v * 128, 128), 128)],
            out_sem.at[j, v],
        )

    def ready(j, carry):
        for v in range(1, 7):
            send(j, v).start()
        return carry

    lax.fori_loop(0, early_blocks(), ready, 0)

    def late(j, carry):
        def one(v, inner):
            unit(raw.at[j + 1], streamed.at[j], v, lanes_of)

            @pl.when(v > 1)
            def _():
                send(j, v - 1).start()

            return inner

        return lax.fori_loop(0, 8, one, carry)

    lax.fori_loop(early_blocks(), 3, late, 0)
    for j in range(3):
        for v in range(1, 7):
            send(j, v).wait()


def third_kernel(neighbours, migration, mine, low_a, low_b, high_a, high_b, got_in, held, out_in,
                 out, got, streamed, fx, fu, fd, rows, tags, table, tag_sem, got_sem, side_sem, row_sem):
    del got_in, held, out_in
    pair = (device_index() >> 1) << 3
    leaver, moving = leaver_of(migration)
    lane = lax.broadcasted_iota(jnp.int32, (8, 128), 1)
    sub = lax.broadcasted_iota(jnp.int32, (8, 128), 0)

    tag_copies = [pltpu.make_async_copy(got.at[TAG_AT, pl.ds(0, 1)], tags.at[pl.ds(0, 1)], tag_sem.at[0])]
    for k, ref in enumerate((low_a, low_b, high_a, high_b)):
        tag_copies.append(pltpu.make_async_copy(ref.at[5, pl.ds(0, 1)], tags.at[pl.ds(k + 1, 1)], tag_sem.at[k + 1]))
    for cp in tag_copies:
        cp.start()

    for s, ref in enumerate((mine, got)):
        fx[s] = ref[pl.ds(FX_AT, 10)]
        fu[s] = ref[pl.ds(FU_AT, 5)]
        fd[s] = ref[pl.ds(FD_AT, 5)]
    for s in range(2):
        fu[2 + s] = (low_a, low_b)[s][pl.ds(0, 5)]
        fd[2 + s] = (high_a, high_b)[s][pl.ds(0, 5)]

    @pl.when(jnp.logical_not(moving))
    def _():
        def keep(n, carry):
            got[n] = mine[n]
            return carry

        lax.fori_loop(0, FX_AT, keep, 0)

    for cp in tag_copies:
        cp.wait()
    for p in range(4):
        table[migration[leaver if p == 0 else staying(p - 1, leaver)] & 7] = p
        for k, (start, source) in enumerate(((0, 1), (8, 2), (8, 3), (16, 2), (16, 3))):
            table[start + (tags[k, 32 * p].astype(jnp.int32) & 7)] = 4 * source + p

    def find(b, k, beside):
        slot = neighbours[b, k]
        code = table[(slot & 7) + jnp.where((slot >> 3) << 3 == pair, 0, beside)]
        return code >> 2, code & 3

    def with_row(now, where, step_x, k, column):
        src, p = where
        home, start = (0, 0) if step_x == 1 else (7, 4)
        x = fx[src, 2 * k + column // 4, pl.ds(8 * (column % 4), 8), :]
        return jnp.where(sub == home, pltpu.roll(x, (home + 8 - start - p) & 7, 0), now)

    def patch_columns(b, xs, at):
        corners = {
            (1, 1): find(b, 5, 8), (-1, 1): find(b, 6, 8),
            (-1, -1): find(b, 4, 16), (1, -1): find(b, 7, 16),
        }
        for high in (0, 1):
            flow = -1 if high else 1
            comps, faces, home = (YD, fd, 3) if high else (YU, fu, 0)
            source = find(b, 2 if high else 3, 16 if high else 8)

            def tile(where, i, part):
                src, p = where
                return pltpu.roll(faces[src, i, pl.ds(8 * part, 8), :], (32 * (home + 4 - p)) & 127, 1)

            edge = (lane >= 96) if high else (lane < 32)
            for c in range(1, 19):
                step_x, step_y, _ = VELOCITY[c]
                in_y = step_y == flow
                if in_y:
                    i = comps.index(c)
                    tiles = [tile(source, i, part) for part in range(4)]
                    if step_x == 1:
                        near = [tile(corners[1, step_y], i, 3)] + tiles
                        near = [pltpu.roll(t, 1, 0) for t in near]
                        tiles = [jnp.where(sub == 0, near[q], near[q + 1]) for q in range(4)]
                    elif step_x == -1:
                        near = tiles + [tile(corners[-1, step_y], i, 0)]
                        near = [pltpu.roll(t, 7, 0) for t in near]
                        tiles = [jnp.where(sub == 7, near[q + 1], near[q]) for q in range(4)]
                for part in range(4):
                    in_x = (step_x == 1 and part == 0) or (step_x == -1 and part == 3)
                    if not in_y and not in_x:
                        continue
                    ref = at(c, part, high)
                    now = ref[...]
                    if in_x:
                        k = (XP if step_x == 1 else XM).index(c)
                        now = with_row(now, xs[step_x], step_x, k, 7 * high)
                    if in_y:
                        now = jnp.where(edge, tiles[part], now)
                    ref[...] = now

    xs = {1: find(leaver, 1, 0), -1: find(leaver, 0, 0)}
    patch_columns(leaver, xs, lambda c, part, high: got.at[19 * 7 * high + c, pl.ds(8 * part, 8), :])
    for step_x, comps in ((1, XP), (-1, XM)):
        for k, c in enumerate(comps):
            for v in range(1, 7):
                ref = got.at[19 * v + c, pl.ds(0 if step_x == 1 else 24, 8), :]
                ref[...] = with_row(ref[...], xs[step_x], step_x, k, v)

    def send(v):
        return pltpu.make_async_copy(
            got.at[pl.ds(19 * v, 19)], out.at[leaver, :, :, pl.ds(128 * v, 128)], got_sem.at[v]
        )

    for v in range(8):
        send(v).start()

    def send_sides(j):
        b = staying(j, leaver)
        return [
            pltpu.make_async_copy(
                streamed.at[j, :, 1 + 7 * high, pl.ds(8, 32), :],
                out.at[b, :, :, pl.ds(896 * high, 128)],
                side_sem.at[j, high],
            )
            for high in range(2)
        ] + [
            pltpu.make_async_copy(
                rows.at[j, last, :, pl.ds(7 * last, 1), :],
                out.at[b, pl.ds(1, 14), pl.ds(31 * last, 1), pl.ds(128, 768)],
                row_sem.at[j, last],
            )
            for last in range(2)
        ]

    def finish_block(j, carry):
        b = staying(j, leaver)
        xs = {1: find(b, 1, 0), -1: find(b, 0, 0)}
        patch_columns(b, xs, lambda c, part, high: streamed.at[j, c, 1 + 7 * high, pl.ds(8 + 8 * part, 8), :])
        for last, step_x, comps in ((0, 1, XP), (1, -1, XM)):
            for c in range(1, 15):
                for v in range(1, 7):
                    now = streamed[j, c, v + 1, pl.ds(8 + 24 * last, 8), :]
                    if c in comps:
                        now = with_row(now, xs[step_x], step_x, comps.index(c), v)
                    rows[j, last, c - 1, :, pl.ds(128 * (v - 1), 128)] = now
        for cp in send_sides(j):
            cp.start()
        return carry

    lax.fori_loop(0, 3, finish_block, 0)
    for j in range(3):
        for cp in send_sides(j):
            cp.wait()
    for v in range(8):
        send(v).wait()


def route(shift, cross):
    count = lax.axis_size("gx") * lax.axis_size("gy")
    return [(d, ((d + shift) % count) ^ cross) for d in range(count)]


def on_device(populations, solid_share, migration, neighbours):
    populations = pltpu.with_memory_space_constraint(populations, pltpu.HBM)
    solid_share = pltpu.with_memory_space_constraint(solid_share, pltpu.HBM)
    migration = pltpu.with_memory_space_constraint(migration, pltpu.HBM)
    neighbours = pltpu.with_memory_space_constraint(neighbours, pltpu.HBM)
    dma = pltpu.SemaphoreType.DMA
    mib = 2**20
    stream_shape = pltpu.VMEM((3, 19, 10, 48, 128), F32)
    mate_shape = pltpu.VMEM((MATE, 32, 128), F32)
    halo_shape = pltpu.VMEM((6, 32, 128), F32)
    out_shape = jax.ShapeDtypeStruct((4, 19, 32, 1024), F32)
    raw, streamed, mate, rise, fall = pl.pallas_call(
        first_kernel,
        name="faces_and_leaver",
        out_shape=(pltpu.VMEM((4, 20, 32, 1024), F32), stream_shape, mate_shape, halo_shape, halo_shape),
        in_specs=[SMEM, HBM, HBM],
        out_specs=(VMEM,) * 5,
        scratch_shapes=[pltpu.VMEM((19, 10, 48, 128), F32), dma((4,)), dma((4,)), dma((8,))],
        compiler_params=pltpu.CompilerParams(vmem_limit_bytes=LIMITS[0] * mib),
        cost_estimate=pl.CostEstimate(flops=20_000_000, bytes_accessed=12_000_000, transcendentals=0),
    )(migration, populations, solid_share)

    axes = ("gx", "gy")
    low_a = lax.ppermute(rise, axes, route(2, 0))
    low_b = lax.ppermute(rise, axes, route(2, 1))
    high_a = lax.ppermute(fall, axes, route(-2, 0))
    high_b = lax.ppermute(fall, axes, route(-2, 1))
    got = lax.ppermute(mate, axes, route(0, 1))

    out, streamed = pl.pallas_call(
        second_kernel,
        name="staying_blocks",
        out_shape=(out_shape, stream_shape),
        in_specs=[SMEM, VMEM, VMEM, VMEM],
        out_specs=(HBM, VMEM),
        input_output_aliases={2: 1},
        scratch_shapes=[dma((3, 8))],
        compiler_params=pltpu.CompilerParams(vmem_limit_bytes=LIMITS[1] * mib),
        cost_estimate=pl.CostEstimate(flops=30_000_000, bytes_accessed=16_000_000, transcendentals=0),
    )(migration, raw, streamed, rise)

    out, _, _ = pl.pallas_call(
        third_kernel,
        name="patch_boundaries",
        out_shape=(out_shape, mate_shape, stream_shape),
        in_specs=[SMEM, SMEM] + [VMEM] * 7 + [HBM],
        out_specs=(HBM, VMEM, VMEM),
        input_output_aliases={9: 0, 7: 1, 8: 2},
        scratch_shapes=[
            pltpu.VMEM((2, 10, 32, 128), F32),
            pltpu.VMEM((4, 5, 32, 128), F32),
            pltpu.VMEM((4, 5, 32, 128), F32),
            pltpu.VMEM((3, 2, 14, 8, 768), F32),
            pltpu.SMEM((5, 128), F32),
            pltpu.SMEM((24,), jnp.int32),
            dma((5,)), dma((8,)), dma((3, 2)), dma((3, 2)),
        ],
        compiler_params=pltpu.CompilerParams(vmem_limit_bytes=LIMITS[2] * mib),
        cost_estimate=pl.CostEstimate(flops=1_000_000, bytes_accessed=8_000_000, transcendentals=0),
    )(neighbours, migration, mate, low_a, low_b, high_a, high_b, got, streamed, out)
    return out


def solution(mesh):
    return jax.shard_map(
        on_device,
        mesh=mesh,
        in_specs=(
            P(("gx", "gy"), None, None, None),
            P(("gx", "gy"), None, None),
            P(("gx", "gy")),
            P(("gx", "gy"), None),
        ),
        out_specs=P(("gx", "gy"), None, None, None),
        check_vma=False,
    )
```

time: 38.6 us -> 36.2 us (0.938)
  Pallas kernels: 22.2 us -> 18.8 us
  waiting for transfers between devices: 1.88 us -> 5.24 us
  local copies, waits for them, and re-layouts: 2.23 us -> 0 us
    pallas_call x3, Pallas kernels: 22.2 us -> 18.8 us  [the longest x1 9.31 us: on_device(): pl.pallas_call(first_kernel, name='faces_and_leaver', out_shape=(pltpu.VM...]
    ppermute x1, waiting for transfers between devices: 0.01 us -> 3.13 us  [on_device(): low_b = lax.ppermute(rise, axes, route(2, 1))]
    unnamed x10 -> x0, local copies, waits for them, and re-layouts: 2.23 us -> none
  transfers between devices with their start and end apart: 5 -> 5, of which waited for: 1 -> 2; matrix products, arithmetic and copies ran while one was open for 0% -> 0% of each run, Pallas kernels for 24% -> 16%
where the time goes in v1:
time: 36.2 us; the launch traced here: 36.1 us
  Pallas kernels  18.8 us (52%)
  starting transfers between devices  12 us (33%)
  waiting for transfers between devices  5.24 us (14%)
    pallas_call x1, Pallas kernels, on_device(): pl.pallas_call(first_kernel, name='faces_and_leaver', out_shape=(pltpu.VM...  9.31 us
    ppermute x1, starting transfers between devices, on_device(): high_b = lax.ppermute(fall, axes, route(-2, 1))  8.45 us
    pallas_call x1, Pallas kernels, on_device(): pl.pallas_call(second_kernel, name='staying_blocks', out_shape=(out_shape...  5.68 us
    pallas_call x1, Pallas kernels, on_device(): pl.pallas_call(third_kernel, name='patch_boundaries', out_shape=(out_shap...  3.81 us
    ppermute x1, waiting for transfers between devices, on_device(): low_b = lax.ppermute(rise, axes, route(2, 1))  3.13 us
    ppermute x1, waiting for transfers between devices, on_device(): low_a = lax.ppermute(rise, axes, route(2, 0))  2.11 us
    ppermute x1, starting transfers between devices, on_device(): low_b = lax.ppermute(rise, axes, route(2, 1))  1.95 us
    ppermute x1, starting transfers between devices, on_device(): got = lax.ppermute(mate, axes, route(0, 1))  1.5 us
  transfers between devices with their start and end apart: 5, of which 2 were waited for; matrix products, arithmetic and copies ran while one was open for 0% of the time, Pallas kernels for 16%

profile of v1, /device:TPU:1, one launch (start us, length us, event | category | flops | bytes accessed | tf_op | source)
XLA Modules:
  0.0 36.1 jit_solution(4896609960085743411)
XLA Ops:
  0.0 9.3 %faces_and_leaver.1 = (f32[4,20,32,1024]{3,2,1,0:T(8,128)S(1)}, f32[3,19,10,48,128]{4,3,2,1,0:T(8,128)S(1)}, f32[173,32,128]{2,1,0:T(8,128)S(1)}, f32[6,32,128]{2,1,0:T(8,128)S(1)}, f32[6,32,128]{2,1,0:T(8,128)S(1)}) custom-call(s32[4]{0:T(128)} %migration.5, f32[4,19,32,1024]{3,2,1,0:T(8,128)} %pop.1, f32[4,32,1024]{2,1,0:T(8,128)} %share.1), custom_call_target="tpu_custom_call" | custom-call | flops 20000000 | bytes 12000000 | tf_op jit(solution)/shard_map/faces_and_leaver/pallas_call | solution.py:470
  9.3 1.5 %collective-permute-start.4 = (f32[173,32,128]{2,1,0:T(8,128)S(1)}, f32[173,32,128]{2,1,0:T(8,128)S(1)}, u32[]{:S(2)}, u32[]{:S(2)}) collective-permute-start(f32[173,32,128]{2,1,0:T(8,128)S(1)} %get-tuple-element.13.mine), channel_id=1, source_target_pairs={{0,1},{1,0},{2,3},{3,2},{4,5},{5,4},{6,7},{7,6},{8,9},{9,8},{10,11... | collective-permute-start | bytes 8503304 | tf_op jit(solution)/shard_map/ppermute | solution.py:486
  10.8 8.5 %collective-permute-start.3 = (f32[6,32,128]{2,1,0:T(8,128)S(1)}, f32[6,32,128]{2,1,0:T(8,128)S(1)}, u32[]{:S(2)}, u32[]{:S(2)}) collective-permute-start(f32[6,32,128]{2,1,0:T(8,128)S(1)} %get-tuple-element.15), channel_id=1, source_target_pairs={{0,127},{1,126},{2,1},{3,0},{4,3},{5,2},{6,5},{7,4},{8,7},{9,6},{1... | collective-permute-start | bytes 294920 | tf_op jit(solution)/shard_map/ppermute | solution.py:485
  19.3 0.1 collective-permute-start.2
  19.4 1.9 %collective-permute-start.1 = (f32[6,32,128]{2,1,0:T(8,128)S(1)}, f32[6,32,128]{2,1,0:T(8,128)S(1)}, u32[]{:S(2)}, u32[]{:S(2)}) collective-permute-start(f32[6,32,128]{2,1,0:T(8,128)S(1)} %get-tuple-element.14.after), channel_id=1, source_target_pairs={{0,3},{1,2},{2,5},{3,4},{4,7},{5,6},{6,9},{7,8},{8,11},{9,10},{10,... | collective-permute-start | bytes 294920 | tf_op jit(solution)/shard_map/ppermute | solution.py:483
  21.3 0.0 collective-permute-start
  21.3 5.7 %staying_blocks.1 = (f32[4,19,32,1024]{3,2,1,0:T(8,128)}, f32[3,19,10,48,128]{4,3,2,1,0:T(8,128)S(1)}) custom-call(s32[4]{0:T(128)} %migration.5, f32[4,20,32,1024]{3,2,1,0:T(8,128)S(1)} %get-tuple-element.16.raw, f32[3,19,10,48,128]{4,3,2,1,0:T(8,128)S(1)} %get-tuple-element.17.held, ...), custom_call_target="tpu_custom_call", output_to_operand_aliasing={{1}: (2, {})} | custom-call | flops 30000000 | bytes 16000000 | tf_op jit(solution)/shard_map/staying_blocks/pallas_call | solution.py:488
  27.0 0.0 collective-permute-done.3.high_b
  27.0 0.0 collective-permute-done.2.high_a
  27.1 3.1 %collective-permute-done.1.low_b = f32[6,32,128]{2,1,0:T(8,128)S(1)} collective-permute-done((f32[6,32,128]{2,1,0:T(8,128)S(1)}, f32[6,32,128]{2,1,0:T(8,128)S(1)}, u32[]{:S(2)}, u32[]{:S(2)}) %collective-permute-start.1) | collective-permute-done | bytes 98336 | tf_op jit(solution)/shard_map/ppermute | solution.py:483
  30.2 2.1 %collective-permute-done.low_a = f32[6,32,128]{2,1,0:T(8,128)S(1)} collective-permute-done((f32[6,32,128]{2,1,0:T(8,128)S(1)}, f32[6,32,128]{2,1,0:T(8,128)S(1)}, u32[]{:S(2)}, u32[]{:S(2)}) %collective-permute-start) | collective-permute-done | bytes 98336 | tf_op jit(solution)/shard_map/ppermute | solution.py:482
  32.3 0.0 collective-permute-done.4.got_in
  32.3 3.8 %patch_boundaries.1 = (f32[4,19,32,1024]{3,2,1,0:T(8,128)}, f32[173,32,128]{2,1,0:T(8,128)S(1)}, f32[3,19,10,48,128]{4,3,2,1,0:T(8,128)S(1)}) custom-call(s32[4,8]{1,0:T(4,128)} %neighbours.1, s32[4]{0:T(128)} %migration.5, f32[173,32,128]{2,1,0:T(8,128)S(1)} %get-tuple-element.13.mine, ...), custom_call_target="tpu_custom_call", output_to_operand_aliasing={{0}: (9, {}), {1}: (7, {}), {2}: (8, {})} | custom-call | flops 1000000 | bytes 8000000 | tf_op jit(solution)/shard_map/patch_boundaries/pallas_call | solution.py:500
Async XLA Ops:
  9.3 23.0 %collective-permute-start.4 = (f32[173,32,128]{2,1,0:T(8,128)S(1)}, f32[173,32,128]{2,1,0:T(8,128)S(1)}, u32[]{:S(2)}, u32[]{:S(2)}) collective-permute-start(f32[173,32,128]{2,1,0:T(8,128)S(1)} %get-tuple-element.13.mine), channel_id=1, source_target_pairs={{0,1},{1,0},{2,3},{3,2},{4,5},{5,4},{6,7},{7,6},{8,9},{9,8},{10,11... | collective-permute-start | bytes 8503304 | tf_op jit(solution)/shard_map/ppermute | solution.py:486
  10.8 16.2 %collective-permute-start.3 = (f32[6,32,128]{2,1,0:T(8,128)S(1)}, f32[6,32,128]{2,1,0:T(8,128)S(1)}, u32[]{:S(2)}, u32[]{:S(2)}) collective-permute-start(f32[6,32,128]{2,1,0:T(8,128)S(1)} %get-tuple-element.15), channel_id=1, source_target_pairs={{0,127},{1,126},{2,1},{3,0},{4,3},{5,2},{6,5},{7,4},{8,7},{9,6},{1... | collective-permute-start | bytes 294920 | tf_op jit(solution)/shard_map/ppermute | solution.py:485
  19.3 7.8 %collective-permute-start.2 = (f32[6,32,128]{2,1,0:T(8,128)S(1)}, f32[6,32,128]{2,1,0:T(8,128)S(1)}, u32[]{:S(2)}, u32[]{:S(2)}) collective-permute-start(f32[6,32,128]{2,1,0:T(8,128)S(1)} %get-tuple-element.15), channel_id=1, source_target_pairs={{0,126},{1,127},{2,0},{3,1},{4,2},{5,3},{6,4},{7,5},{8,6},{9,7},{1... | collective-permute-start | bytes 294920 | tf_op jit(solution)/shard_map/ppermute | solution.py:484
  19.4 10.8 %collective-permute-start.1 = (f32[6,32,128]{2,1,0:T(8,128)S(1)}, f32[6,32,128]{2,1,0:T(8,128)S(1)}, u32[]{:S(2)}, u32[]{:S(2)}) collective-permute-start(f32[6,32,128]{2,1,0:T(8,128)S(1)} %get-tuple-element.14.after), channel_id=1, source_target_pairs={{0,3},{1,2},{2,5},{3,4},{4,7},{5,6},{6,9},{7,8},{8,11},{9,10},{10,... | collective-permute-start | bytes 294920 | tf_op jit(solution)/shard_map/ppermute | solution.py:483
  21.3 10.9 %collective-permute-start = (f32[6,32,128]{2,1,0:T(8,128)S(1)}, f32[6,32,128]{2,1,0:T(8,128)S(1)}, u32[]{:S(2)}, u32[]{:S(2)}) collective-permute-start(f32[6,32,128]{2,1,0:T(8,128)S(1)} %get-tuple-element.14.after), channel_id=1, source_target_pairs={{0,2},{1,3},{2,4},{3,5},{4,6},{5,7},{6,8},{7,9},{8,10},{9,11},{10,... | collective-permute-start | bytes 294920 | tf_op jit(solution)/shard_map/ppermute | solution.py:482

commit v2 on v1

v2 whole, which is shorter than its diff:
```python
import functools

import jax
import jax.numpy as jnp
from jax import lax
from jax.experimental import pallas as pl
from jax.experimental.pallas import tpu as pltpu
from jax.sharding import PartitionSpec as P

VELOCITY = [
    (0, 0, 0), (1, 0, 0), (-1, 0, 0), (0, 1, 0), (0, -1, 0), (0, 0, 1), (0, 0, -1),
    (1, 1, 0), (-1, -1, 0), (1, -1, 0), (-1, 1, 0), (1, 0, 1), (-1, 0, -1), (1, 0, -1),
    (-1, 0, 1), (0, 1, 1), (0, -1, -1), (0, 1, -1), (0, -1, 1),
]
XP = [1, 7, 9, 11, 13]
XM = [2, 8, 10, 12, 14]
YU = [3, 7, 10, 15, 17]
YD = [4, 8, 9, 16, 18]
F32 = jnp.float32
HBM = pl.BlockSpec(memory_space=pltpu.HBM)
VMEM = pl.BlockSpec(memory_space=pltpu.VMEM)
SMEM = pl.BlockSpec(memory_space=pltpu.SMEM)
FX_AT, FU_AT, FD_AT, TAG_AT, MATE = 152, 162, 167, 172, 173
HALO = 21


def collide(f, share):
    q = 1.0 - share
    s = [None] * 19
    d = [None] * 19
    for i in range(1, 19, 2):
        s[i] = f[i] + f[i + 1]
        d[i] = f[i] - f[i + 1]
    dxy, exy = s[7] + s[9], s[7] - s[9]
    dxz, exz = s[11] + s[13], s[11] - s[13]
    dyz, eyz = s[15] + s[17], s[15] - s[17]
    sx = (s[1] + s[3]) + s[5]
    sd = (dxy + dxz) + dyz
    rho = (f[0] + sx) + sd
    axy, bxy = d[7] + d[9], d[7] - d[9]
    axz, bxz = d[11] + d[13], d[11] - d[13]
    ayz, byz = d[15] + d[17], d[15] - d[17]
    tx, ty, tz = axy + axz, bxy + ayz, bxz + byz
    jx, jy, jz = d[1] + tx, d[3] + ty, d[5] + tz
    r = pl.reciprocal(rho, approx=True)
    r = r * (2.0 - rho * r)
    vx, vy, vz = jx * r, jy * r, jz * r
    ux, uy, uz = jx * vx, jy * vy, jz * vz
    j2 = (ux + uy) + uz
    iso_a = (-173.0 / 1800.0) * f[0] + (-4.0 / 45.0) * sx + ((-29.0 / 600.0) * sd + (197.0 / 1800.0) * j2)
    iso_d = (-23.0 / 900.0) * f[0] + (-1.0 / 36.0) * sx + ((-19.0 / 300.0) * sd + (-103.0 / 900.0) * j2)
    iso_0 = (53.0 / 60.0) * f[0] + (-7.0 / 15.0) * sx + ((-5.0 / 12.0) * sd + 0.65 * j2)

    def axis_even(x, dd, u):
        return q * ((11.0 / 15.0) * x + (-1.0 / 30.0) * dd + ((-23.0 / 60.0) * u + iso_a))

    def plane_even(x, dd, u):
        return q * ((-1.0 / 30.0) * x + (23.0 / 60.0) * dd + ((5.0 / 24.0) * u + iso_d))

    q4 = 0.4 * q
    q2 = 0.2 * q
    qm = 0.2475 * q
    ex, ey, ez = axis_even(s[1], dyz, ux), axis_even(s[3], dxz, uy), axis_even(s[5], dxy, uz)
    pyz, pxz, pxy = plane_even(s[1], dyz, ux), plane_even(s[3], dxz, uy), plane_even(s[5], dxy, uz)
    hxy, hxz, hyz = q4 * (exy - jx * vy), q4 * (exz - jx * vz), q4 * (eyz - jy * vz)
    hx = q2 * ((d[1] + d[1]) - tx)
    hy = q2 * ((d[3] + d[3]) - ty)
    hz = q2 * ((d[5] + d[5]) - tz)
    gx, gy, gz = 0.25 * hx, 0.25 * hy, 0.25 * hz
    mx, my, mz = qm * (axy - axz), qm * (ayz - bxy), qm * (bxz - byz)
    axy_o, bxy_o = mx - gx, -(my + gy)
    axz_o, bxz_o = -(mx + gx), mz - gz
    ayz_o, byz_o = my - gy, -(mz + gz)
    odd = {
        1: hx, 3: hy, 5: hz,
        7: axy_o + bxy_o, 9: axy_o - bxy_o,
        11: axz_o + bxz_o, 13: axz_o - bxz_o,
        15: ayz_o + byz_o, 17: ayz_o - byz_o,
    }
    even = {
        1: ex, 3: ey, 5: ez,
        7: pxy + hxy, 9: pxy - hxy,
        11: pxz + hxz, 13: pxz - hxz,
        15: pyz + hyz, 17: pyz - hyz,
    }
    post = [None] * 19
    post[0] = f[0] - q * iso_0
    for i in range(1, 19, 2):
        w = odd[i] + share * d[i]
        post[i] = (f[i] - even[i]) - w
        post[i + 1] = (f[i + 1] - even[i]) + w
    return post


def lane_tables():
    lane = lax.broadcasted_iota(jnp.int32, (8, 128), 1)
    tables = {}
    for step_y in (-1, 0, 1):
        for step_z in (-1, 1):
            tables[step_y, step_z] = ((lane - 32 * step_y) & 96) | ((lane - step_z) & 31)
    return lane, tables


def turn(x, step_y, step_z, tables):
    if step_z:
        return jnp.take_along_axis(x, tables[step_y, step_z], axis=1)
    return pltpu.roll(x, (32 * step_y) % 128, 1) if step_y else x


ORDER = [5, 11, 14, 6, 12, 13, 15, 17, 16, 18, 3, 7, 10, 4, 8, 9]


def collide_part(source, column, part, stage, result):
    at = pl.ds(pl.multiple_of(column * 128, 128), 128)
    rows = pl.ds(8 * part, 8)
    post = collide([source[c, rows, at] for c in range(19)], source[19, rows, at])
    for c in range(3):
        result[c, column + 1, pl.ds(8 + 8 * part + VELOCITY[c][0], 8), :] = post[c]
    for c in range(3, 19):
        stage[c - 3, rows, :] = post[c]


def turn_all(stage, column, result, lanes_of):
    lane, tables = lanes_of
    for c in ORDER:
        step_x, step_y, step_z = VELOCITY[c]
        out = (lane < 32) if step_y == 1 else (lane >= 96)
        for part in range(4):
            value = turn(stage[c - 3, pl.ds(8 * part, 8), :], step_y, step_z, tables)
            to = pl.ds(8 + 8 * part + step_x, 8)
            if step_y == 0:
                result[c, column + 1, to, :] = value
            else:
                pltpu.store(result.at[c, column + 1, to, :], value, mask=jnp.logical_not(out))
                pltpu.store(result.at[c, column + 1 + step_y, to, :], value, mask=out)


def process(source, result, stage, lanes_of, after):
    def one(v, carry):
        for part in range(4):
            collide_part(source, v, part, stage, result)
        turn_all(stage, v, result, lanes_of)
        after(v)
        return carry

    lax.fori_loop(0, 8, one, 0)


def device_index():
    return lax.axis_index("gx") * lax.axis_size("gy") + lax.axis_index("gy")


def leaver_of(migration):
    base = device_index() * 4
    leaver = jnp.int32(0)
    moving = jnp.bool_(False)
    for b in (3, 2, 1, 0):
        away = migration[b] != base + b
        leaver = jnp.where(away, b, leaver)
        moving = jnp.logical_or(moving, away)
    return leaver, moving


def staying(j, leaver):
    return j + (j >= leaver).astype(jnp.int32)


def early_blocks():
    return jnp.where(device_index() < 2, 3, 2).astype(jnp.int32)


def block_at(p, leaver):
    return jnp.where(p == 0, leaver, staying(p - 1, leaver))


def first_kernel(migration, neighbours, pop, share, raw, streamed, mate, stage, pop_sem, share_sem, mate_sem):
    lanes_of = lane_tables()
    lane, tables = lanes_of
    segment = lane >> 5
    sub = lax.broadcasted_iota(jnp.int32, (8, 128), 0)
    leaver, _ = leaver_of(migration)

    def load(p):
        b = block_at(p, leaver)
        return (
            pltpu.make_async_copy(pop.at[b], raw.at[p, pl.ds(0, 19)], pop_sem.at[p]),
            pltpu.make_async_copy(share.at[b], raw.at[p, 19], share_sem.at[p]),
        )

    for p in range(4):
        for cp in load(p):
            cp.start()

    pair = (device_index() >> 1) << 3
    tag = jnp.zeros((8, 128), F32)
    for p in range(4):
        slot = migration[block_at(p, leaver)]
        above = (((neighbours[p, 2] >> 3) << 3) != pair).astype(jnp.int32)
        value = jnp.where(sub == 0, jnp.full((8, 128), slot, jnp.int32), jnp.full((8, 128), above, jnp.int32))
        tag = jnp.where(segment == p, value.astype(F32), tag)
    mate[TAG_AT, pl.ds(0, 8), :] = tag

    def faces(p):
        mine = segment == p
        for part in range(4):
            rows = pl.ds(8 * part, 8)

            def ends(c):
                return jnp.where(lane < 64, raw[p, c, rows, pl.ds(0, 128)], raw[p, c, rows, pl.ds(896, 128)])

            post = collide([ends(c) for c in range(19)], ends(19))
            for comps, at, shift in ((YU, FU_AT, 32 * p + 32), (YD, FD_AT, 32 * p)):
                for i, c in enumerate(comps):
                    value = pltpu.roll(turn(post[c], 0, VELOCITY[c][2], tables), shift & 127, 1)
                    pltpu.store(mate.at[at + i, rows, :], value, mask=mine)

        for end, comps in ((0, XP), (1, XM)):

            def packed(c):
                got = None
                for v in range(8):
                    x = raw[p, c, pl.ds(24 - 24 * end, 8), pl.ds(128 * v, 128)]
                    shift = (v + 1 - end) % 8
                    x = pltpu.roll(x, shift, 0) if shift else x
                    got = x if got is None else jnp.where(sub == v, x, got)
                return got

            post = collide([packed(c) for c in range(19)], packed(19))
            for i, c in enumerate(comps):
                _, step_y, step_z = VELOCITY[c]
                value = turn(post[c], step_y, step_z, tables)
                if step_y:
                    out = (lane < 32) if step_y == 1 else (lane >= 96)
                    value = jnp.where(out, pltpu.roll(value, step_y % 8, 0), value)
                mate[FX_AT + 5 * end + i, pl.ds(pl.multiple_of(8 * p, 8), 8), :] = value

    def hand(v):
        return pltpu.make_async_copy(
            streamed.at[0, :, v + 1, pl.ds(8, 32), :], mate.at[pl.ds(19 * v, 19)], mate_sem.at[v]
        )

    def work(p, carry):
        for cp in load(p):
            cp.wait()
        faces(p)

        @pl.when(p == 0)
        def _():
            def after(v):
                @pl.when(v > 0)
                def _():
                    hand(v - 1).start()

            process(raw.at[0], streamed.at[0], stage, lanes_of, after)
            hand(7).start()

        return carry

    lax.fori_loop(0, 4, work, 0)
    for v in range(8):
        hand(v).wait()


def staying_kernel(late, migration, raw, held, after, *refs):
    out, streamed, stage, out_sem = refs[-4:]
    lanes_of = lane_tables()
    leaver, _ = leaver_of(migration)

    def send(p, v):
        return pltpu.make_async_copy(
            streamed.at[p, :, v + 1, pl.ds(8, 32), :],
            out.at[block_at(p, leaver), :, :, pl.ds(pl.multiple_of(v * 128, 128), 128)],
            out_sem.at[p - 1, v],
        )

    def block(p, carry):
        def after(v):
            @pl.when(v > 1)
            def _():
                send(p, v - 1).start()

        process(raw.at[p], streamed.at[p], stage, lanes_of, after)
        return carry

    def finish(p, carry):
        for v in range(1, 7):
            send(p, v).wait()
        return carry

    middle = early_blocks() + 1
    low, high = (middle, 4) if late else (1, middle)
    lax.fori_loop(low, high, block, 0)
    lax.fori_loop(low, high, finish, 0)


def select_kernel(migration, mine, got, after, rise, fall, faces, tags, table, places, tag_sem):
    del after
    leaver, _ = leaver_of(migration)
    lane = lax.broadcasted_iota(jnp.int32, (8, 128), 1)
    segment = lane >> 5
    tag_copies = [
        pltpu.make_async_copy(ref.at[TAG_AT, pl.ds(0, 2)], tags.at[s], tag_sem.at[s]) for s, ref in enumerate((mine, got))
    ]
    for cp in tag_copies:
        cp.start()
    for s, ref in enumerate((mine, got)):
        for high, at in enumerate((FU_AT, FD_AT)):
            faces[s, high] = ref[pl.ds(at, 5)]
    for cp in tag_copies:
        cp.wait()
    for s in range(2):
        for p in range(4):
            table[tags[s, 0, 32 * p].astype(jnp.int32) & 7] = 4 * s + p
    own = (device_index() & 1) * 4
    ups, downs = jnp.int32(0), jnp.int32(0)
    for s in range(2):
        for b in range(4):
            up = tags[s, 1, 32 * b].astype(jnp.int32)
            slot = (own ^ (4 * s)) + b
            places[jnp.where(up == 1, ups, 4 + downs)] = slot
            ups, downs = ups + up, downs + 1 - up
    pair = (device_index() >> 1) << 3
    for high, halo in enumerate((rise, fall)):
        tag = jnp.zeros((8, 128), F32)
        where = []
        for m in range(4):
            slot = places[4 * high + m]
            code = table[slot]
            where.append((code >> 2, code & 3))
            tag = jnp.where(segment == m, jnp.full((8, 128), pair + slot, jnp.int32).astype(F32), tag)
        halo[20] = tag
        for i in range(5):
            for part in range(4):
                got_tile = None
                for m, (src, p) in enumerate(where):
                    x = pltpu.roll(faces[src, high, i, pl.ds(8 * part, 8), :], (32 * (4 + m - p)) & 127, 1)
                    got_tile = x if m == 0 else jnp.where(segment == m, x, got_tile)
                halo[4 * i + part] = got_tile


def third_kernel(neighbours, migration, mine, high, low, got_in, held, out_in,
                 out, got, streamed, fx, fu, fd, rows, tags, table, tag_sem, got_sem, side_sem, row_sem):
    del got_in, held, out_in
    pair = (device_index() >> 1) << 3
    leaver, moving = leaver_of(migration)
    lane = lax.broadcasted_iota(jnp.int32, (8, 128), 1)
    sub = lax.broadcasted_iota(jnp.int32, (8, 128), 0)

    tag_copies = [pltpu.make_async_copy(got.at[TAG_AT, pl.ds(0, 1)], tags.at[pl.ds(0, 1)], tag_sem.at[0])]
    for k, ref in enumerate((low, high)):
        tag_copies.append(pltpu.make_async_copy(ref.at[20, pl.ds(0, 1)], tags.at[pl.ds(k + 1, 1)], tag_sem.at[k + 1]))
    for cp in tag_copies:
        cp.start()

    for s, ref in enumerate((mine, got)):
        fx[s] = ref[pl.ds(FX_AT, 10)]
        fu[s] = ref[pl.ds(FU_AT, 5)]
        fd[s] = ref[pl.ds(FD_AT, 5)]
    for n in range(20):
        fu[2, n // 4, pl.ds(8 * (n % 4), 8), :] = low[n]
        fd[2, n // 4, pl.ds(8 * (n % 4), 8), :] = high[n]

    @pl.when(jnp.logical_not(moving))
    def _():
        def keep(n, carry):
            got[n] = mine[n]
            return carry

        lax.fori_loop(0, FX_AT, keep, 0)

    for cp in tag_copies:
        cp.wait()
    for p in range(4):
        table[migration[leaver if p == 0 else staying(p - 1, leaver)] & 7] = p
        for k, (start, source) in enumerate(((0, 1), (8, 2), (16, 2))):
            table[start + (tags[k, 32 * p].astype(jnp.int32) & 7)] = 4 * source + p

    def find(b, k, beside):
        slot = neighbours[b, k]
        code = table[(slot & 7) + jnp.where((slot >> 3) << 3 == pair, 0, beside)]
        return code >> 2, code & 3

    def with_row(now, where, step_x, k, column):
        src, p = where
        home, start = (0, 0) if step_x == 1 else (7, 5)
        x = fx[src, start + k, pl.ds(pl.multiple_of(8 * p, 8), 8), :]
        return jnp.where(sub == home, pltpu.roll(x, (home - column) % 8, 0), now)

    def patch_columns(b, xs, at):
        corners = {
            (1, 1): find(b, 5, 8), (-1, 1): find(b, 6, 8),
            (-1, -1): find(b, 4, 16), (1, -1): find(b, 7, 16),
        }
        for high in (0, 1):
            flow = -1 if high else 1
            comps, faces, home = (YD, fd, 3) if high else (YU, fu, 0)
            source = find(b, 2 if high else 3, 16 if high else 8)

            def tile(where, i, part):
                src, p = where
                return pltpu.roll(faces[src, i, pl.ds(8 * part, 8), :], (32 * (home + 4 - p)) & 127, 1)

            edge = (lane >= 96) if high else (lane < 32)
            for c in range(1, 19):
                step_x, step_y, _ = VELOCITY[c]
                in_y = step_y == flow
                if in_y:
                    i = comps.index(c)
                    tiles = [tile(source, i, part) for part in range(4)]
                    if step_x == 1:
                        near = [tile(corners[1, step_y], i, 3)] + tiles
                        near = [pltpu.roll(t, 1, 0) for t in near]
                        tiles = [jnp.where(sub == 0, near[q], near[q + 1]) for q in range(4)]
                    elif step_x == -1:
                        near = tiles + [tile(corners[-1, step_y], i, 0)]
                        near = [pltpu.roll(t, 7, 0) for t in near]
                        tiles = [jnp.where(sub == 7, near[q + 1], near[q]) for q in range(4)]
                for part in range(4):
                    in_x = (step_x == 1 and part == 0) or (step_x == -1 and part == 3)
                    if not in_y and not in_x:
                        continue
                    ref = at(c, part, high)
                    now = ref[...]
                    if in_x:
                        k = (XP if step_x == 1 else XM).index(c)
                        now = with_row(now, xs[step_x], step_x, k, 7 * high)
                    if in_y:
                        now = jnp.where(edge, tiles[part], now)
                    ref[...] = now

    xs = {1: find(leaver, 1, 0), -1: find(leaver, 0, 0)}
    patch_columns(leaver, xs, lambda c, part, high: got.at[19 * 7 * high + c, pl.ds(8 * part, 8), :])
    for step_x, comps in ((1, XP), (-1, XM)):
        for k, c in enumerate(comps):
            for v in range(1, 7):
                ref = got.at[19 * v + c, pl.ds(0 if step_x == 1 else 24, 8), :]
                ref[...] = with_row(ref[...], xs[step_x], step_x, k, v)

    def send(v):
        return pltpu.make_async_copy(
            got.at[pl.ds(19 * v, 19)], out.at[leaver, :, :, pl.ds(128 * v, 128)], got_sem.at[v]
        )

    for v in range(8):
        send(v).start()

    def send_sides(j):
        b = staying(j, leaver)
        return [
            pltpu.make_async_copy(
                streamed.at[j + 1, :, 1 + 7 * high, pl.ds(8, 32), :],
                out.at[b, :, :, pl.ds(896 * high, 128)],
                side_sem.at[j, high],
            )
            for high in range(2)
        ] + [
            pltpu.make_async_copy(
                rows.at[j, last, :, pl.ds(7 * last, 1), :],
                out.at[b, pl.ds(1, 14), pl.ds(31 * last, 1), pl.ds(128, 768)],
                row_sem.at[j, last],
            )
            for last in range(2)
        ]

    def finish_block(j, carry):
        b = staying(j, leaver)
        xs = {1: find(b, 1, 0), -1: find(b, 0, 0)}
        patch_columns(b, xs, lambda c, part, high: streamed.at[j + 1, c, 1 + 7 * high, pl.ds(8 + 8 * part, 8), :])
        for last, step_x, comps in ((0, 1, XP), (1, -1, XM)):
            for c in range(1, 15):
                for v in range(1, 7):
                    now = streamed[j + 1, c, v + 1, pl.ds(8 + 24 * last, 8), :]
                    if c in comps:
                        now = with_row(now, xs[step_x], step_x, comps.index(c), v)
                    rows[j, last, c - 1, :, pl.ds(128 * (v - 1), 128)] = now
        for cp in send_sides(j):
            cp.start()
        return carry

    lax.fori_loop(0, 3, finish_block, 0)
    for j in range(3):
        for cp in send_sides(j):
            cp.wait()
    for v in range(8):
        send(v).wait()


def route(shift, cross):
    count = lax.axis_size("gx") * lax.axis_size("gy")
    return [(d, ((d + shift) % count) ^ cross) for d in range(count)]


def on_device(populations, solid_share, migration, neighbours):
    populations = pltpu.with_memory_space_constraint(populations, pltpu.HBM)
    solid_share = pltpu.with_memory_space_constraint(solid_share, pltpu.HBM)
    migration = pltpu.with_memory_space_constraint(migration, pltpu.HBM)
    neighbours = pltpu.with_memory_space_constraint(neighbours, pltpu.HBM)
    dma = pltpu.SemaphoreType.DMA
    mib = 2**20
    stage = pltpu.VMEM((16, 32, 128), F32)
    stream_shape = pltpu.VMEM((4, 19, 10, 48, 128), F32)
    mate_shape = pltpu.VMEM((MATE, 32, 128), F32)
    halo_shape = pltpu.VMEM((HALO, 8, 128), F32)
    out_shape = jax.ShapeDtypeStruct((4, 19, 32, 1024), F32)

    def params(limit):
        return pltpu.CompilerParams(vmem_limit_bytes=limit * mib)

    def cost(flops, data):
        return pl.CostEstimate(flops=flops, bytes_accessed=data, transcendentals=0)

    raw, streamed, mate = pl.pallas_call(
        first_kernel,
        name="faces_and_leaver",
        out_shape=(pltpu.VMEM((4, 20, 32, 1024), F32), stream_shape, mate_shape),
        in_specs=[SMEM, SMEM, HBM, HBM],
        out_specs=(VMEM,) * 3,
        scratch_shapes=[stage, dma((4,)), dma((4,)), dma((8,))],
        compiler_params=params(4),
        cost_estimate=cost(20_000_000, 12_000_000),
    )(migration, neighbours, populations, solid_share)

    axes = ("gx", "gy")
    got = lax.ppermute(mate, axes, route(0, 1))

    out, streamed = pl.pallas_call(
        functools.partial(staying_kernel, False),
        name="early_blocks",
        out_shape=(out_shape, stream_shape),
        in_specs=[SMEM, VMEM, VMEM, VMEM],
        out_specs=(HBM, VMEM),
        input_output_aliases={2: 1},
        scratch_shapes=[stage, dma((3, 8))],
        compiler_params=params(4),
        cost_estimate=cost(30_000_000, 16_000_000),
    )(migration, raw, streamed, mate)

    rise, fall = pl.pallas_call(
        select_kernel,
        name="select_faces",
        out_shape=(halo_shape, halo_shape),
        in_specs=[SMEM, VMEM, VMEM, VMEM],
        out_specs=(VMEM, VMEM),
        scratch_shapes=[
            pltpu.VMEM((2, 2, 5, 32, 128), F32),
            pltpu.SMEM((2, 2, 128), F32),
            pltpu.SMEM((8,), jnp.int32),
            pltpu.SMEM((8,), jnp.int32),
            dma((2,)),
        ],
        compiler_params=params(4),
        cost_estimate=cost(1_000_000, 1_000_000),
    )(migration, mate, got, streamed)
    low = lax.ppermute(rise, axes, route(2, 0))
    high = lax.ppermute(fall, axes, route(-2, 0))

    out, streamed = pl.pallas_call(
        functools.partial(staying_kernel, True),
        name="late_blocks",
        out_shape=(out_shape, stream_shape),
        in_specs=[SMEM, VMEM, VMEM, VMEM, HBM],
        out_specs=(HBM, VMEM),
        input_output_aliases={4: 0, 2: 1},
        scratch_shapes=[stage, dma((3, 8))],
        compiler_params=params(4),
        cost_estimate=cost(30_000_000, 16_000_000),
    )(migration, raw, streamed, rise, out)

    out, _, _ = pl.pallas_call(
        third_kernel,
        name="patch_boundaries",
        out_shape=(out_shape, mate_shape, stream_shape),
        in_specs=[SMEM, SMEM] + [VMEM] * 5 + [HBM],
        out_specs=(HBM, VMEM, VMEM),
        input_output_aliases={7: 0, 5: 1, 6: 2},
        scratch_shapes=[
            pltpu.VMEM((2, 10, 32, 128), F32),
            pltpu.VMEM((3, 5, 32, 128), F32),
            pltpu.VMEM((3, 5, 32, 128), F32),
            pltpu.VMEM((3, 2, 14, 8, 768), F32),
            pltpu.SMEM((3, 128), F32),
            pltpu.SMEM((24,), jnp.int32),
            dma((3,)), dma((8,)), dma((3, 2)), dma((3, 2)),
        ],
        compiler_params=params(8),
        cost_estimate=cost(1_000_000, 8_000_000),
    )(neighbours, migration, mate, high, low, got, streamed, out)
    return out


def solution(mesh):
    return jax.shard_map(
        on_device,
        mesh=mesh,
        in_specs=(
            P(("gx", "gy"), None, None, None),
            P(("gx", "gy"), None, None),
            P(("gx", "gy")),
            P(("gx", "gy"), None),
        ),
        out_specs=P(("gx", "gy"), None, None, None),
        check_vma=False,
    )
```

time: 36.2 us -> 36.4 us (level)
  starting transfers between devices: 12 us -> 8.11 us
  waiting for transfers between devices: 5.24 us -> 8.35 us
  Pallas kernels: 18.8 us -> 19.7 us
    pallas_call x1 -> x3, Pallas kernels: 5.68 us -> 9.9 us  [the longest x1 7.45 us: on_device(): pl.pallas_call(functools.partial(staying_kernel, False), name='early_bloc...]
    ppermute x4 -> x2, starting transfers between devices: 10.5 us -> 6.61 us  [the longest x1 6.6 us: on_device(): high = lax.ppermute(fall, axes, route(-2, 0))]
    pallas_call x1, Pallas kernels: 9.31 us -> 6.05 us  [on_device(): pl.pallas_call(first_kernel, name='faces_and_leaver', out_shape=(pltpu.VM...]
    ppermute x4 -> x2, waiting for transfers between devices: 5.24 us -> 8.34 us  [the longest x1 7.31 us: on_device(): low = lax.ppermute(rise, axes, route(2, 0))]
  transfers between devices with their start and end apart: 5 -> 3, of which waited for: 2 -> 2; matrix products, arithmetic and copies ran while one was open for 0% -> 0% of each run, Pallas kernels for 16% -> 23%
where the time goes in v2:
time: 36.4 us; the launch traced here: 36.2 us
  Pallas kernels  19.7 us (54%)
  waiting for transfers between devices  8.35 us (23%)
  starting transfers between devices  8.11 us (22%)
    pallas_call x1, Pallas kernels, on_device(): pl.pallas_call(functools.partial(staying_kernel, False), name='early_bloc...  7.45 us
    ppermute x1, waiting for transfers between devices, on_device(): low = lax.ppermute(rise, axes, route(2, 0))  7.31 us
    ppermute x1, starting transfers between devices, on_device(): high = lax.ppermute(fall, axes, route(-2, 0))  6.6 us
    pallas_call x1, Pallas kernels, on_device(): pl.pallas_call(first_kernel, name='faces_and_leaver', out_shape=(pltpu.VM...  6.05 us
    pallas_call x1, Pallas kernels, on_device(): pl.pallas_call(third_kernel, name='patch_boundaries', out_shape=(out_shap...  3.75 us
    pallas_call x1, Pallas kernels, on_device(): pl.pallas_call(select_kernel, name='select_faces', out_shape=(halo_shape,...  1.55 us
    ppermute x1, starting transfers between devices, on_device(): got = lax.ppermute(mate, axes, route(0, 1))  1.5 us
    ppermute x1, waiting for transfers between devices, on_device(): high = lax.ppermute(fall, axes, route(-2, 0))  1.03 us
  transfers between devices with their start and end apart: 3, of which 2 were waited for; matrix products, arithmetic and copies ran while one was open for 0% of the time, Pallas kernels for 23%

profile of v2, /device:TPU:1, one launch (start us, length us, event | category | flops | bytes accessed | tf_op | source)
XLA Modules:
  0.0 36.2 jit_solution(2985273211830877541)
XLA Ops:
  0.0 6.1 %faces_and_leaver.1 = (f32[4,20,32,1024]{3,2,1,0:T(8,128)S(1)}, f32[4,19,10,48,128]{4,3,2,1,0:T(8,128)S(1)}, f32[173,32,128]{2,1,0:T(8,128)S(1)}) custom-call(s32[4]{0:T(128)} %migration.9, s32[4,8]{1,0:T(4,128)} %neighbours.3, f32[4,19,32,1024]{3,2,1,0:T(8,128)} %pop.1, f32[4,32,1024]{2,1,0:T(8,128)} %share.1), custom_call_target="tpu_custom_call" | custom-call | flops 20000000 | bytes 12000000 | tf_op jit(solution)/shard_map/faces_and_leaver/pallas_call | solution.py:512
  6.1 1.5 %collective-permute-start = (f32[173,32,128]{2,1,0:T(8,128)S(1)}, f32[173,32,128]{2,1,0:T(8,128)S(1)}, u32[]{:S(2)}, u32[]{:S(2)}) collective-permute-start(f32[173,32,128]{2,1,0:T(8,128)S(1)} %get-tuple-element.15.after.mine), channel_id=1, source_target_pairs={{0,1},{1,0},{2,3},{3,2},{4,5},{5,4},{6,7},{7,6},{8,9},{9,8},{10,11... | collective-permute-start | bytes 8503304 | tf_op jit(solution)/shard_map/ppermute | solution.py:524
  7.6 7.5 %early_blocks.1 = (f32[4,19,32,1024]{3,2,1,0:T(8,128)}, f32[4,19,10,48,128]{4,3,2,1,0:T(8,128)S(1)}) custom-call(s32[4]{0:T(128)} %migration.9, f32[4,20,32,1024]{3,2,1,0:T(8,128)S(1)} %get-tuple-element.16.raw, f32[4,19,10,48,128]{4,3,2,1,0:T(8,128)S(1)} %get-tuple-element.17.held, ...), custom_call_target="tpu_custom_call", output_to_operand_aliasing={{1}: (2, {})} | custom-call | flops 30000000 | bytes 16000000 | tf_op jit(solution)/shard_map/early_blocks/pallas_call | solution.py:526
  15.0 0.0 collective-permute-done.got.got_in
  15.0 1.6 %select_faces.1 = (f32[21,8,128]{2,1,0:T(8,128)S(1)}, f32[21,8,128]{2,1,0:T(8,128)S(1)}) custom-call(s32[4]{0:T(128)} %migration.9, f32[173,32,128]{2,1,0:T(8,128)S(1)} %get-tuple-element.15.after.mine, f32[173,32,128]{2,1,0:T(8,128)S(1)} %collective-permute-done.got.got_in, f32[4,19,10,48,128]{4,3,2,1,0:T(8,128)S(1)} %get-tuple-element.18.after.held), custom_call_target="tpu_custom_call" | custom-call | flops 1000000 | bytes 1000000 | tf_op jit(solution)/shard_map/select_faces/pallas_call | solution.py:538
  16.6 6.6 %collective-permute-start.1 = (f32[21,8,128]{2,1,0:T(8,128)S(1)}, f32[21,8,128]{2,1,0:T(8,128)S(1)}, u32[]{:S(2)}, u32[]{:S(2)}) collective-permute-start(f32[21,8,128]{2,1,0:T(8,128)S(1)} %get-tuple-element.19), channel_id=1, source_target_pairs={{0,126},{1,127},{2,0},{3,1},{4,2},{5,3},{6,4},{7,5},{8,6},{9,7},{1... | collective-permute-start | bytes 258056 | tf_op jit(solution)/shard_map/ppermute | solution.py:555
  23.2 0.0 collective-permute-start.2
  23.2 0.9 %late_blocks.1 = (f32[4,19,32,1024]{3,2,1,0:T(8,128)}, f32[4,19,10,48,128]{4,3,2,1,0:T(8,128)S(1)}) custom-call(s32[4]{0:T(128)} %migration.9, f32[4,20,32,1024]{3,2,1,0:T(8,128)S(1)} %get-tuple-element.16.raw, f32[4,19,10,48,128]{4,3,2,1,0:T(8,128)S(1)} %get-tuple-element.18.after.held, ...), custom_call_target="tpu_custom_call", output_to_operand_aliasing={{0}: (4, {}), {1}: (2, {})} | custom-call | flops 30000000 | bytes 16000000 | tf_op jit(solution)/shard_map/late_blocks/pallas_call | solution.py:557
  24.1 1.0 %collective-permute-done.1.high = f32[21,8,128]{2,1,0:T(8,128)S(1)} collective-permute-done((f32[21,8,128]{2,1,0:T(8,128)S(1)}, f32[21,8,128]{2,1,0:T(8,128)S(1)}, u32[]{:S(2)}, u32[]{:S(2)}) %collective-permute-start.1) | collective-permute-done | bytes 86048 | tf_op jit(solution)/shard_map/ppermute | solution.py:555
  25.1 7.3 %collective-permute-done.2.low = f32[21,8,128]{2,1,0:T(8,128)S(1)} collective-permute-done((f32[21,8,128]{2,1,0:T(8,128)S(1)}, f32[21,8,128]{2,1,0:T(8,128)S(1)}, u32[]{:S(2)}, u32[]{:S(2)}) %collective-permute-start.2) | collective-permute-done | bytes 86048 | tf_op jit(solution)/shard_map/ppermute | solution.py:554
  32.5 3.8 %patch_boundaries.1 = (f32[4,19,32,1024]{3,2,1,0:T(8,128)}, f32[173,32,128]{2,1,0:T(8,128)S(1)}, f32[4,19,10,48,128]{4,3,2,1,0:T(8,128)S(1)}) custom-call(s32[4,8]{1,0:T(4,128)} %neighbours.3, s32[4]{0:T(128)} %migration.9, f32[173,32,128]{2,1,0:T(8,128)S(1)} %get-tuple-element.15.after.mine, ...), custom_call_target="tpu_custom_call", output_to_operand_aliasing={{0}: (7, {}), {1}: (5, {}), {2}: (6, {})} | custom-call | flops 1000000 | bytes 8000000 | tf_op jit(solution)/shard_map/patch_boundaries/pallas_call | solution.py:569
Async XLA Ops:
  6.1 9.0 %collective-permute-start = (f32[173,32,128]{2,1,0:T(8,128)S(1)}, f32[173,32,128]{2,1,0:T(8,128)S(1)}, u32[]{:S(2)}, u32[]{:S(2)}) collective-permute-start(f32[173,32,128]{2,1,0:T(8,128)S(1)} %get-tuple-element.15.after.mine), channel_id=1, source_target_pairs={{0,1},{1,0},{2,3},{3,2},{4,5},{5,4},{6,7},{7,6},{8,9},{9,8},{10,11... | collective-permute-start | bytes 8503304 | tf_op jit(solution)/shard_map/ppermute | solution.py:524
  16.6 8.6 %collective-permute-start.1 = (f32[21,8,128]{2,1,0:T(8,128)S(1)}, f32[21,8,128]{2,1,0:T(8,128)S(1)}, u32[]{:S(2)}, u32[]{:S(2)}) collective-permute-start(f32[21,8,128]{2,1,0:T(8,128)S(1)} %get-tuple-element.19), channel_id=1, source_target_pairs={{0,126},{1,127},{2,0},{3,1},{4,2},{5,3},{6,4},{7,5},{8,6},{9,7},{1... | collective-permute-start | bytes 258056 | tf_op jit(solution)/shard_map/ppermute | solution.py:555
  23.2 9.3 %collective-permute-start.2 = (f32[21,8,128]{2,1,0:T(8,128)S(1)}, f32[21,8,128]{2,1,0:T(8,128)S(1)}, u32[]{:S(2)}, u32[]{:S(2)}) collective-permute-start(f32[21,8,128]{2,1,0:T(8,128)S(1)} %get-tuple-element.20.after), channel_id=1, source_target_pairs={{0,2},{1,3},{2,4},{3,5},{4,6},{5,7},{6,8},{7,9},{8,10},{9,11},{10,... | collective-permute-start | bytes 258056 | tf_op jit(solution)/shard_map/ppermute | solution.py:554

commit v3 on v2

--- a/solution.py
+++ b/solution.py
@@ -166,14 +166,14 @@
 
 
 def early_blocks():
-    return jnp.where(device_index() < 2, 3, 2).astype(jnp.int32)
+    return jnp.where((device_index() >> 1) & 3 == 0, 3, 2).astype(jnp.int32)
 
 
 def block_at(p, leaver):
     return jnp.where(p == 0, leaver, staying(p - 1, leaver))
 
 
-def first_kernel(migration, neighbours, pop, share, raw, streamed, mate, stage, pop_sem, share_sem, mate_sem):
+def first_kernel(migration, neighbours, pop, share, raw, mate, leaving, stage, pop_sem, share_sem, mate_sem):
     lanes_of = lane_tables()
     lane, tables = lanes_of
     segment = lane >> 5
@@ -236,7 +236,7 @@
 
     def hand(v):
         return pltpu.make_async_copy(
-            streamed.at[0, :, v + 1, pl.ds(8, 32), :], mate.at[pl.ds(19 * v, 19)], mate_sem.at[v]
+            leaving.at[:, v + 1, pl.ds(8, 32), :], mate.at[pl.ds(19 * v, 19)], mate_sem.at[v]
         )
 
     def work(p, carry):
@@ -251,7 +251,7 @@
                 def _():
                     hand(v - 1).start()
 
-            process(raw.at[0], streamed.at[0], stage, lanes_of, after)
+            process(raw.at[0], leaving, stage, lanes_of, after)
             hand(7).start()
 
         return carry
@@ -261,25 +261,27 @@
         hand(v).wait()
 
 
-def staying_kernel(late, migration, raw, held, after, *refs):
-    out, streamed, stage, out_sem = refs[-4:]
+def column_send(streamed, out, out_sem, leaver, p, v):
+    return pltpu.make_async_copy(
+        streamed.at[p - 1, :, v + 1, pl.ds(8, 32), :],
+        out.at[block_at(p, leaver), :, :, pl.ds(pl.multiple_of(v * 128, 128), 128)],
+        out_sem.at[p - 1, v],
+    )
+
+
+def early_kernel(migration, raw, after, out, streamed, stage, out_sem):
+    del after
     lanes_of = lane_tables()
     leaver, _ = leaver_of(migration)
-
-    def send(p, v):
-        return pltpu.make_async_copy(
-            streamed.at[p, :, v + 1, pl.ds(8, 32), :],
-            out.at[block_at(p, leaver), :, :, pl.ds(pl.multiple_of(v * 128, 128), 128)],
-            out_sem.at[p - 1, v],
-        )
+    send = functools.partial(column_send, streamed, out, out_sem, leaver)
 
     def block(p, carry):
-        def after(v):
+        def after_column(v):
             @pl.when(v > 1)
             def _():
                 send(p, v - 1).start()
 
-        process(raw.at[p], streamed.at[p], stage, lanes_of, after)
+        process(raw.at[p], streamed.at[p - 1], stage, lanes_of, after_column)
         return carry
 
     def finish(p, carry):
@@ -287,10 +289,128 @@
             send(p, v).wait()
         return carry
 
+    end = early_blocks() + 1
+    lax.fori_loop(1, end, block, 0)
+    lax.fori_loop(1, end, finish, 0)
+
+
+def late_kernel(neighbours, migration, raw, held, mine, got_in, after, out_in, out, streamed, got,
+                stage, fx, rows, tags, table, tag_sem, out_sem, got_sem, row_sem):
+    del held, got_in, after, out_in
+    lanes_of = lane_tables()
+    leaver, moving = leaver_of(migration)
+    sub = lax.broadcasted_iota(jnp.int32, (8, 128), 0)
+    send = functools.partial(column_send, streamed, out, out_sem, leaver)
+    tag_copy = pltpu.make_async_copy(got.at[TAG_AT, pl.ds(0, 1)], tags, tag_sem)
+    tag_copy.start()
+    for s, ref in enumerate((mine, got)):
+        fx[s] = ref[pl.ds(FX_AT, 10)]
+
+    @pl.when(jnp.logical_not(moving))
+    def _():
+        def keep(n, carry):
+            got[n] = mine[n]
+            return carry
+
+        lax.fori_loop(0, FX_AT, keep, 0)
+
+    tag_copy.wait()
+    for p in range(4):
+        table[migration[block_at(p, leaver)] & 7] = p
+        table[tags[0, 32 * p].astype(jnp.int32) & 7] = 4 + p
+
+    def incoming(b):
+        found = {}
+        for step_x, k in ((1, 1), (-1, 0)):
+            code = table[neighbours[b, k] & 7]
+            found[step_x] = (code >> 2, code & 3)
+        return found
+
+    def with_row(now, where, step_x, k, column):
+        src, p = where
+        home, start = (0, 0) if step_x == 1 else (7, 5)
+        x = fx[src, start + k, pl.ds(pl.multiple_of(8 * p, 8), 8), :]
+        return jnp.where(sub == home, pltpu.roll(x, (home - column) & 7, 0), now)
+
+    def patch_column(xs, v, at):
+        for step_x, comps in ((1, XP), (-1, XM)):
+            for k, c in enumerate(comps):
+                ref = at(c, 0 if step_x == 1 else 24)
+                ref[...] = with_row(ref[...], xs[step_x], step_x, k, v)
+
+    def streamed_at(p, v):
+        return lambda c, row: streamed.at[p - 1, c, v + 1, pl.ds(8 + row, 8), :]
+
+    xs = incoming(leaver)
+
+    def arrived(v):
+        return pltpu.make_async_copy(
+            got.at[pl.ds(19 * v, 19)], out.at[leaver, :, :, pl.ds(128 * v, 128)], got_sem.at[v]
+        )
+
+    for v in range(8):
+        patch_column(xs, v, lambda c, row: got.at[19 * v + c, pl.ds(row, 8), :])
+        if 0 < v < 7:
+            arrived(v).start()
+
+    def send_rows(p):
+        return [
+            pltpu.make_async_copy(
+                rows.at[p - 1, last, :, pl.ds(7 * last, 1), :],
+                out.at[block_at(p, leaver), pl.ds(1, 14), pl.ds(31 * last, 1), pl.ds(128, 768)],
+                row_sem.at[p - 1, last],
+            )
+            for last in range(2)
+        ]
+
+    def written(p, carry):
+        xs = incoming(block_at(p, leaver))
+        for last, step_x, comps in ((0, 1, XP), (1, -1, XM)):
+            for c in range(1, 15):
+                for v in range(1, 7):
+                    now = streamed[p - 1, c, v + 1, pl.ds(8 + 24 * last, 8), :]
+                    if c in comps:
+                        now = with_row(now, xs[step_x], step_x, comps.index(c), v)
+                    rows[p - 1, last, c - 1, :, pl.ds(128 * (v - 1), 128)] = now
+        for cp in send_rows(p):
+            cp.start()
+        for v in (0, 7):
+            patch_column(xs, v, streamed_at(p, v))
+        return carry
+
+    def remaining(p, carry):
+        xs = incoming(block_at(p, leaver))
+
+        def after_column(v):
+            @pl.when(v > 0)
+            def _():
+                patch_column(xs, v - 1, streamed_at(p, v - 1))
+
+            @pl.when(v > 1)
+            def _():
+                send(p, v - 1).start()
+
+        process(raw.at[p], streamed.at[p - 1], stage, lanes_of, after_column)
+        patch_column(xs, 7, streamed_at(p, 7))
+        return carry
+
+    def finish(p, carry):
+        for v in range(1, 7):
+            send(p, v).wait()
+        return carry
+
+    def finish_rows(p, carry):
+        for cp in send_rows(p):
+            cp.wait()
+        return carry
+
     middle = early_blocks() + 1
-    low, high = (middle, 4) if late else (1, middle)
-    lax.fori_loop(low, high, block, 0)
-    lax.fori_loop(low, high, finish, 0)
+    lax.fori_loop(1, middle, written, 0)
+    lax.fori_loop(middle, 4, remaining, 0)
+    lax.fori_loop(1, middle, finish_rows, 0)
+    lax.fori_loop(middle, 4, finish, 0)
+    for v in range(1, 7):
+        arrived(v).wait()
 
 
 def select_kernel(migration, mine, got, after, rise, fall, faces, tags, table, places, tag_sem):
@@ -338,40 +458,33 @@
                 halo[4 * i + part] = got_tile
 
 
-def third_kernel(neighbours, migration, mine, high, low, got_in, held, out_in,
-                 out, got, streamed, fx, fu, fd, rows, tags, table, tag_sem, got_sem, side_sem, row_sem):
-    del got_in, held, out_in
+def last_kernel(neighbours, migration, mine, low, high, got, streamed_in, out_in,
+                out, streamed, fu, fd, columns, tags, table, tag_sem, got_sem, side_sem):
+    del streamed_in, out_in
     pair = (device_index() >> 1) << 3
-    leaver, moving = leaver_of(migration)
+    leaver, _ = leaver_of(migration)
     lane = lax.broadcasted_iota(jnp.int32, (8, 128), 1)
     sub = lax.broadcasted_iota(jnp.int32, (8, 128), 0)
 
-    tag_copies = [pltpu.make_async_copy(got.at[TAG_AT, pl.ds(0, 1)], tags.at[pl.ds(0, 1)], tag_sem.at[0])]
-    for k, ref in enumerate((low, high)):
-        tag_copies.append(pltpu.make_async_copy(ref.at[20, pl.ds(0, 1)], tags.at[pl.ds(k + 1, 1)], tag_sem.at[k + 1]))
+    tag_copies = [
+        pltpu.make_async_copy(ref, tags.at[pl.ds(k, 1)], tag_sem.at[k])
+        for k, ref in enumerate((got.at[TAG_AT, pl.ds(0, 1)], low.at[20, pl.ds(0, 1)], high.at[20, pl.ds(0, 1)]))
+    ]
     for cp in tag_copies:
         cp.start()
-
     for s, ref in enumerate((mine, got)):
-        fx[s] = ref[pl.ds(FX_AT, 10)]
         fu[s] = ref[pl.ds(FU_AT, 5)]
         fd[s] = ref[pl.ds(FD_AT, 5)]
     for n in range(20):
         fu[2, n // 4, pl.ds(8 * (n % 4), 8), :] = low[n]
         fd[2, n // 4, pl.ds(8 * (n % 4), 8), :] = high[n]
-
-    @pl.when(jnp.logical_not(moving))
-    def _():
-        def keep(n, carry):
-            got[n] = mine[n]
-            return carry
-
-        lax.fori_loop(0, FX_AT, keep, 0)
+    for high_side in range(2):
+        columns[high_side] = got[pl.ds(19 * 7 * high_side, 19)]
 
     for cp in tag_copies:
         cp.wait()
     for p in range(4):
-        table[migration[leaver if p == 0 else staying(p - 1, leaver)] & 7] = p
+        table[migration[block_at(p, leaver)] & 7] = p
         for k, (start, source) in enumerate(((0, 1), (8, 2), (16, 2))):
             table[start + (tags[k, 32 * p].astype(jnp.int32) & 7)] = 4 * source + p
 
@@ -380,109 +493,69 @@
         code = table[(slot & 7) + jnp.where((slot >> 3) << 3 == pair, 0, beside)]
         return code >> 2, code & 3
 
-    def with_row(now, where, step_x, k, column):
-        src, p = where
-        home, start = (0, 0) if step_x == 1 else (7, 5)
-        x = fx[src, start + k, pl.ds(pl.multiple_of(8 * p, 8), 8), :]
-        return jnp.where(sub == home, pltpu.roll(x, (home - column) % 8, 0), now)
-
-    def patch_columns(b, xs, at):
+    def patch_columns(b, at):
         corners = {
             (1, 1): find(b, 5, 8), (-1, 1): find(b, 6, 8),
             (-1, -1): find(b, 4, 16), (1, -1): find(b, 7, 16),
         }
-        for high in (0, 1):
-            flow = -1 if high else 1
-            comps, faces, home = (YD, fd, 3) if high else (YU, fu, 0)
-            source = find(b, 2 if high else 3, 16 if high else 8)
+        for upper in (0, 1):
+            comps, faces, home = (YD, fd, 3) if upper else (YU, fu, 0)
+            source = find(b, 2 if upper else 3, 16 if upper else 8)
+            edge = (lane >= 96) if upper else (lane < 32)
 
             def tile(where, i, part):
                 src, p = where
                 return pltpu.roll(faces[src, i, pl.ds(8 * part, 8), :], (32 * (home + 4 - p)) & 127, 1)
 
-            edge = (lane >= 96) if high else (lane < 32)
-            for c in range(1, 19):
+            for i, c in enumerate(comps):
                 step_x, step_y, _ = VELOCITY[c]
-                in_y = step_y == flow
-                if in_y:
-                    i = comps.index(c)
-                    tiles = [tile(source, i, part) for part in range(4)]
-                    if step_x == 1:
-                        near = [tile(corners[1, step_y], i, 3)] + tiles
-                        near = [pltpu.roll(t, 1, 0) for t in near]
-                        tiles = [jnp.where(sub == 0, near[q], near[q + 1]) for q in range(4)]
-                    elif step_x == -1:
-                        near = tiles + [tile(corners[-1, step_y], i, 0)]
-                        near = [pltpu.roll(t, 7, 0) for t in near]
-                        tiles = [jnp.where(sub == 7, near[q + 1], near[q]) for q in range(4)]
+                tiles = [tile(source, i, part) for part in range(4)]
+                if step_x == 1:
+                    near = [tile(corners[1, step_y], i, 3)] + tiles
+                    near = [pltpu.roll(t, 1, 0) for t in near]
+                    tiles = [jnp.where(sub == 0, near[q], near[q + 1]) for q in range(4)]
+                elif step_x == -1:
+                    near = tiles + [tile(corners[-1, step_y], i, 0)]
+                    near = [pltpu.roll(t, 7, 0) for t in near]
+                    tiles = [jnp.where(sub == 7, near[q + 1], near[q]) for q in range(4)]
                 for part in range(4):
-                    in_x = (step_x == 1 and part == 0) or (step_x == -1 and part == 3)
-                    if not in_y and not in_x:
-                        continue
-                    ref = at(c, part, high)
-                    now = ref[...]
-                    if in_x:
-                        k = (XP if step_x == 1 else XM).index(c)
-                        now = with_row(now, xs[step_x], step_x, k, 7 * high)
-                    if in_y:
-                        now = jnp.where(edge, tiles[part], now)
-                    ref[...] = now
-
-    xs = {1: find(leaver, 1, 0), -1: find(leaver, 0, 0)}
-    patch_columns(leaver, xs, lambda c, part, high: got.at[19 * 7 * high + c, pl.ds(8 * part, 8), :])
-    for step_x, comps in ((1, XP), (-1, XM)):
-        for k, c in enumerate(comps):
-            for v in range(1, 7):
-                ref = got.at[19 * v + c, pl.ds(0 if step_x == 1 else 24, 8), :]
-                ref[...] = with_row(ref[...], xs[step_x], step_x, k, v)
-
-    def send(v):
+                    ref = at(c, part, upper)
+                    ref[...] = jnp.where(edge, tiles[part], ref[...])
+
+    def send_arrived(upper):
         return pltpu.make_async_copy(
-            got.at[pl.ds(19 * v, 19)], out.at[leaver, :, :, pl.ds(128 * v, 128)], got_sem.at[v]
+            columns.at[upper], out.at[leaver, :, :, pl.ds(896 * upper, 128)], got_sem.at[upper]
         )
 
-    for v in range(8):
-        send(v).start()
-
-    def send_sides(j):
-        b = staying(j, leaver)
+    patch_columns(leaver, lambda c, part, upper: columns.at[upper, c, pl.ds(8 * part, 8), :])
+    for upper in range(2):
+        send_arrived(upper).start()
+
+    def send_sides(p):
         return [
             pltpu.make_async_copy(
-                streamed.at[j + 1, :, 1 + 7 * high, pl.ds(8, 32), :],
-                out.at[b, :, :, pl.ds(896 * high, 128)],
-                side_sem.at[j, high],
+                streamed.at[p - 1, :, 1 + 7 * upper, pl.ds(8, 32), :],
+                out.at[block_at(p, leaver), :, :, pl.ds(896 * upper, 128)],
+                side_sem.at[p - 1, upper],
             )
-            for high in range(2)
-        ] + [
-            pltpu.make_async_copy(
-                rows.at[j, last, :, pl.ds(7 * last, 1), :],
-                out.at[b, pl.ds(1, 14), pl.ds(31 * last, 1), pl.ds(128, 768)],
-                row_sem.at[j, last],
-            )
-            for last in range(2)
+            for upper in range(2)
         ]
 
-    def finish_block(j, carry):
-        b = staying(j, leaver)
-        xs = {1: find(b, 1, 0), -1: find(b, 0, 0)}
-        patch_columns(b, xs, lambda c, part, high: streamed.at[j + 1, c, 1 + 7 * high, pl.ds(8 + 8 * part, 8), :])
-        for last, step_x, comps in ((0, 1, XP), (1, -1, XM)):
-            for c in range(1, 15):
-                for v in range(1, 7):
-                    now = streamed[j + 1, c, v + 1, pl.ds(8 + 24 * last, 8), :]
-                    if c in comps:
-                        now = with_row(now, xs[step_x], step_x, comps.index(c), v)
-                    rows[j, last, c - 1, :, pl.ds(128 * (v - 1), 128)] = now
-        for cp in send_sides(j):
+    def finish_block(p, carry):
+        patch_columns(
+            block_at(p, leaver),
+            lambda c, part, upper: streamed.at[p - 1, c, 1 + 7 * upper, pl.ds(8 + 8 * part, 8), :],
+        )
+        for cp in send_sides(p):
             cp.start()
         return carry
 
-    lax.fori_loop(0, 3, finish_block, 0)
-    for j in range(3):
-        for cp in send_sides(j):
+    lax.fori_loop(1, 4, finish_block, 0)
+    for p in range(1, 4):
+        for cp in send_sides(p):
             cp.wait()
-    for v in range(8):
-        send(v).wait()
+    for upper in range(2):
+        send_arrived(upper).wait()
 
 
 def route(shift, cross):
@@ -498,7 +571,7 @@
     dma = pltpu.SemaphoreType.DMA
     mib = 2**20
     stage = pltpu.VMEM((16, 32, 128), F32)
-    stream_shape = pltpu.VMEM((4, 19, 10, 48, 128), F32)
+    stream_shape = pltpu.VMEM((3, 19, 10, 48, 128), F32)
     mate_shape = pltpu.VMEM((MATE, 32, 128), F32)
     halo_shape = pltpu.VMEM((HALO, 8, 128), F32)
     out_shape = jax.ShapeDtypeStruct((4, 19, 32, 1024), F32)
@@ -509,14 +582,14 @@
     def cost(flops, data):
         return pl.CostEstimate(flops=flops, bytes_accessed=data, transcendentals=0)
 
-    raw, streamed, mate = pl.pallas_call(
+    raw, mate = pl.pallas_call(
         first_kernel,
         name="faces_and_leaver",
-        out_shape=(pltpu.VMEM((4, 20, 32, 1024), F32), stream_shape, mate_shape),
+        out_shape=(pltpu.VMEM((4, 20, 32, 1024), F32), mate_shape),
         in_specs=[SMEM, SMEM, HBM, HBM],
-        out_specs=(VMEM,) * 3,
-        scratch_shapes=[stage, dma((4,)), dma((4,)), dma((8,))],
-        compiler_params=params(4),
+        out_specs=(VMEM,) * 2,
+        scratch_shapes=[pltpu.VMEM((19, 10, 48, 128), F32), stage, dma((4,)), dma((4,)), dma((8,))],
+        compiler_params=params(8),
         cost_estimate=cost(20_000_000, 12_000_000),
     )(migration, neighbours, populations, solid_share)
 
@@ -524,16 +597,15 @@
     got = lax.ppermute(mate, axes, route(0, 1))
 
     out, streamed = pl.pallas_call(
-        functools.partial(staying_kernel, False),
+        early_kernel,
         name="early_blocks",
         out_shape=(out_shape, stream_shape),
-        in_specs=[SMEM, VMEM, VMEM, VMEM],
+        in_specs=[SMEM, VMEM, VMEM],
         out_specs=(HBM, VMEM),
-        input_output_aliases={2: 1},
         scratch_shapes=[stage, dma((3, 8))],
         compiler_params=params(4),
         cost_estimate=cost(30_000_000, 16_000_000),
-    )(migration, raw, streamed, mate)
+    )(migration, raw, mate)
 
     rise, fall = pl.pallas_call(
         select_kernel,
@@ -551,40 +623,46 @@
         compiler_params=params(4),
         cost_estimate=cost(1_000_000, 1_000_000),
     )(migration, mate, got, streamed)
+    high = lax.ppermute(fall, axes, route(-2, 0))
     low = lax.ppermute(rise, axes, route(2, 0))
-    high = lax.ppermute(fall, axes, route(-2, 0))
-
-    out, streamed = pl.pallas_call(
-        functools.partial(staying_kernel, True),
+
+    out, streamed, got = pl.pallas_call(
+        late_kernel,
         name="late_blocks",
-        out_shape=(out_shape, stream_shape),
-        in_specs=[SMEM, VMEM, VMEM, VMEM, HBM],
-        out_specs=(HBM, VMEM),
-        input_output_aliases={4: 0, 2: 1},
-        scratch_shapes=[stage, dma((3, 8))],
-        compiler_params=params(4),
-        cost_estimate=cost(30_000_000, 16_000_000),
-    )(migration, raw, streamed, rise, out)
-
-    out, _, _ = pl.pallas_call(
-        third_kernel,
-        name="patch_boundaries",
-        out_shape=(out_shape, mate_shape, stream_shape),
+        out_shape=(out_shape, stream_shape, mate_shape),
         in_specs=[SMEM, SMEM] + [VMEM] * 5 + [HBM],
         out_specs=(HBM, VMEM, VMEM),
-        input_output_aliases={7: 0, 5: 1, 6: 2},
+        input_output_aliases={7: 0, 3: 1, 5: 2},
         scratch_shapes=[
+            stage,
             pltpu.VMEM((2, 10, 32, 128), F32),
+            pltpu.VMEM((3, 2, 14, 8, 768), F32),
+            pltpu.SMEM((1, 128), F32),
+            pltpu.SMEM((8,), jnp.int32),
+            dma, dma((3, 8)), dma((8,)), dma((3, 2)),
+        ],
+        compiler_params=params(6),
+        cost_estimate=cost(30_000_000, 16_000_000),
+    )(neighbours, migration, raw, streamed, mate, got, fall, out)
+
+    out, _ = pl.pallas_call(
+        last_kernel,
+        name="outer_columns",
+        out_shape=(out_shape, stream_shape),
+        in_specs=[SMEM, SMEM] + [VMEM] * 5 + [HBM],
+        out_specs=(HBM, VMEM),
+        input_output_aliases={7: 0, 6: 1},
+        scratch_shapes=[
             pltpu.VMEM((3, 5, 32, 128), F32),
             pltpu.VMEM((3, 5, 32, 128), F32),
-            pltpu.VMEM((3, 2, 14, 8, 768), F32),
+            pltpu.VMEM((2, 19, 32, 128), F32),
             pltpu.SMEM((3, 128), F32),
             pltpu.SMEM((24,), jnp.int32),
-            dma((3,)), dma((8,)), dma((3, 2)), dma((3, 2)),
+            dma((3,)), dma((2,)), dma((3, 2)),
         ],
-        compiler_params=params(8),
+        compiler_params=params(6),
         cost_estimate=cost(1_000_000, 8_000_000),
-    )(neighbours, migration, mate, high, low, got, streamed, out)
+    )(neighbours, migration, mate, low, high, got, streamed, out)
     return out
 
 

time: 36.4 us -> 29.7 us (0.82)
  waiting for transfers between devices: 8.35 us -> 0.01 us
  Pallas kernels: 19.7 us -> 21 us
    ppermute x1, waiting for transfers between devices: 7.31 us -> 0.01 us  [on_device(): low = lax.ppermute(rise, axes, route(2, 0))]
    pallas_call x3, Pallas kernels: 12.1 us -> 13.3 us  [the longest x1 7.44 us: on_device(): pl.pallas_call(early_kernel, name='early_blocks', out_shape=(out_shape, s...]
    ppermute x1, waiting for transfers between devices: 1.03 us -> 0.01 us  [on_device(): high = lax.ppermute(fall, axes, route(-2, 0))]
  transfers between devices with their start and end apart: 3 -> 3, of which waited for: 2 -> 0; matrix products, arithmetic and copies ran while one was open for 0% -> 0% of each run, Pallas kernels for 23% -> 35%
where the time goes in v3:
time: 29.7 us; the launch traced here: 29.5 us
  Pallas kernels  21 us (71%)
  starting transfers between devices  8.46 us (28%)
    pallas_call x1, Pallas kernels, on_device(): pl.pallas_call(early_kernel, name='early_blocks', out_shape=(out_shape, s...  7.44 us
    ppermute x1, starting transfers between devices, on_device(): high = lax.ppermute(fall, axes, route(-2, 0))  6.88 us
    pallas_call x1, Pallas kernels, on_device(): pl.pallas_call(first_kernel, name='faces_and_leaver', out_shape=(pltpu.VM...  6.08 us
    pallas_call x1, Pallas kernels, on_device(): pl.pallas_call(last_kernel, name='outer_columns', out_shape=(out_shape, s...  2.96 us
    pallas_call x1, Pallas kernels, on_device(): pl.pallas_call(late_kernel, name='late_blocks', out_shape=(out_shape, str...  2.94 us
    pallas_call x1, Pallas kernels, on_device(): pl.pallas_call(select_kernel, name='select_faces', out_shape=(halo_shape,...  1.55 us
    ppermute x1, starting transfers between devices, on_device(): got = lax.ppermute(mate, axes, route(0, 1))  1.5 us
  transfers between devices with their start and end apart: 3, of which 0 were waited for; matrix products, arithmetic and copies ran while one was open for 0% of the time, Pallas kernels for 35%

profile of v3, /device:TPU:1, one launch (start us, length us, event | category | flops | bytes accessed | tf_op | source)
XLA Modules:
  0.0 29.5 jit_solution(12014823318655432070)
XLA Ops:
  0.0 6.1 %faces_and_leaver.1 = (f32[4,20,32,1024]{3,2,1,0:T(8,128)S(1)}, f32[173,32,128]{2,1,0:T(8,128)S(1)}) custom-call(s32[4]{0:T(128)} %migration.9, s32[4,8]{1,0:T(4,128)} %neighbours.5, f32[4,19,32,1024]{3,2,1,0:T(8,128)} %pop.1, f32[4,32,1024]{2,1,0:T(8,128)} %share.1), custom_call_target="tpu_custom_call" | custom-call | flops 20000000 | bytes 12000000 | tf_op jit(solution)/shard_map/faces_and_leaver/pallas_call | solution.py:585
  6.1 1.5 %collective-permute-start = (f32[173,32,128]{2,1,0:T(8,128)S(1)}, f32[173,32,128]{2,1,0:T(8,128)S(1)}, u32[]{:S(2)}, u32[]{:S(2)}) collective-permute-start(f32[173,32,128]{2,1,0:T(8,128)S(1)} %get-tuple-element.15.after.mine), channel_id=1, source_target_pairs={{0,1},{1,0},{2,3},{3,2},{4,5},{5,4},{6,7},{7,6},{8,9},{9,8},{10,11... | collective-permute-start | bytes 8503304 | tf_op jit(solution)/shard_map/ppermute | solution.py:597
  7.6 7.4 %early_blocks.1 = (f32[4,19,32,1024]{3,2,1,0:T(8,128)}, f32[3,19,10,48,128]{4,3,2,1,0:T(8,128)S(1)}) custom-call(s32[4]{0:T(128)} %migration.9, f32[4,20,32,1024]{3,2,1,0:T(8,128)S(1)} %get-tuple-element.16.raw, f32[173,32,128]{2,1,0:T(8,128)S(1)} %get-tuple-element.15.after.mine), custom_call_target="tpu_custom_call" | custom-call | flops 30000000 | bytes 16000000 | tf_op jit(solution)/shard_map/early_blocks/pallas_call | solution.py:599
  15.0 0.0 collective-permute-done.got.got_in
  15.1 1.6 %select_faces.1 = (f32[21,8,128]{2,1,0:T(8,128)S(1)}, f32[21,8,128]{2,1,0:T(8,128)S(1)}) custom-call(s32[4]{0:T(128)} %migration.9, f32[173,32,128]{2,1,0:T(8,128)S(1)} %get-tuple-element.15.after.mine, f32[173,32,128]{2,1,0:T(8,128)S(1)} %collective-permute-done.got.got_in, f32[3,19,10,48,128]{4,3,2,1,0:T(8,128)S(1)} %get-tuple-element.17.after.held), custom_call_target="tpu_custom_call" | custom-call | flops 1000000 | bytes 1000000 | tf_op jit(solution)/shard_map/select_faces/pallas_call | solution.py:610
  16.6 0.1 collective-permute-start.1
  16.7 6.9 %collective-permute-start.2 = (f32[21,8,128]{2,1,0:T(8,128)S(1)}, f32[21,8,128]{2,1,0:T(8,128)S(1)}, u32[]{:S(2)}, u32[]{:S(2)}) collective-permute-start(f32[21,8,128]{2,1,0:T(8,128)S(1)} %get-tuple-element.19.after), channel_id=1, source_target_pairs={{0,126},{1,127},{2,0},{3,1},{4,2},{5,3},{6,4},{7,5},{8,6},{9,7},{1... | collective-permute-start | bytes 258056 | tf_op jit(solution)/shard_map/ppermute | solution.py:626
  23.6 2.9 %late_blocks.1 = (f32[4,19,32,1024]{3,2,1,0:T(8,128)}, f32[3,19,10,48,128]{4,3,2,1,0:T(8,128)S(1)}, f32[173,32,128]{2,1,0:T(8,128)S(1)}) custom-call(s32[4,8]{1,0:T(4,128)} %neighbours.5, s32[4]{0:T(128)} %migration.9, f32[4,20,32,1024]{3,2,1,0:T(8,128)S(1)} %get-tuple-element.16.raw, ...), custom_call_target="tpu_custom_call", output_to_operand_aliasing={{0}: (7, {}), {1}: (3, {}), {2}: (5, {})} | custom-call | flops 30000000 | bytes 16000000 | tf_op jit(solution)/shard_map/late_blocks/pallas_call | solution.py:629
  26.5 0.0 collective-permute-done.1.low
  26.5 0.0 collective-permute-done.2.high
  26.5 3.0 %outer_columns.1 = (f32[4,19,32,1024]{3,2,1,0:T(8,128)}, f32[3,19,10,48,128]{4,3,2,1,0:T(8,128)S(1)}) custom-call(s32[4,8]{1,0:T(4,128)} %neighbours.5, s32[4]{0:T(128)} %migration.9, f32[173,32,128]{2,1,0:T(8,128)S(1)} %get-tuple-element.15.after.mine, f32[21,8,128]{2,1,0:T(8,128)S(1)} %collective-permute-done.1.low, ...), custom_call_target="tpu_custom_call", output_to_operand_aliasing={{0}: (7, {}), {1}: (6, {})} | custom-call | flops 1000000 | bytes 8000000 | tf_op jit(solution)/shard_map/outer_columns/pallas_call | solution.py:648
Async XLA Ops:
  6.1 9.0 %collective-permute-start = (f32[173,32,128]{2,1,0:T(8,128)S(1)}, f32[173,32,128]{2,1,0:T(8,128)S(1)}, u32[]{:S(2)}, u32[]{:S(2)}) collective-permute-start(f32[173,32,128]{2,1,0:T(8,128)S(1)} %get-tuple-element.15.after.mine), channel_id=1, source_target_pairs={{0,1},{1,0},{2,3},{3,2},{4,5},{5,4},{6,7},{7,6},{8,9},{9,8},{10,11... | collective-permute-start | bytes 8503304 | tf_op jit(solution)/shard_map/ppermute | solution.py:597
  16.6 9.9 %collective-permute-start.1 = (f32[21,8,128]{2,1,0:T(8,128)S(1)}, f32[21,8,128]{2,1,0:T(8,128)S(1)}, u32[]{:S(2)}, u32[]{:S(2)}) collective-permute-start(f32[21,8,128]{2,1,0:T(8,128)S(1)} %get-tuple-element.18), channel_id=1, source_target_pairs={{0,2},{1,3},{2,4},{3,5},{4,6},{5,7},{6,8},{7,9},{8,10},{9,11},{10,... | collective-permute-start | bytes 258056 | tf_op jit(solution)/shard_map/ppermute | solution.py:627
  16.7 9.8 %collective-permute-start.2 = (f32[21,8,128]{2,1,0:T(8,128)S(1)}, f32[21,8,128]{2,1,0:T(8,128)S(1)}, u32[]{:S(2)}, u32[]{:S(2)}) collective-permute-start(f32[21,8,128]{2,1,0:T(8,128)S(1)} %get-tuple-element.19.after), channel_id=1, source_target_pairs={{0,126},{1,127},{2,0},{3,1},{4,2},{5,3},{6,4},{7,5},{8,6},{9,7},{1... | collective-permute-start | bytes 258056 | tf_op jit(solution)/shard_map/ppermute | solution.py:626

commit v4 on v3

--- a/solution.py
+++ b/solution.py
@@ -136,14 +136,16 @@
 
 
 def process(source, result, stage, lanes_of, after):
-    def one(v, carry):
-        for part in range(4):
-            collide_part(source, v, part, stage, result)
-        turn_all(stage, v, result, lanes_of)
-        after(v)
-        return carry
-
-    lax.fori_loop(0, 8, one, 0)
+    def some(i, carry):
+        for h in range(4):
+            v = 4 * i + h
+            for part in range(4):
+                collide_part(source, v, part, stage, result)
+            turn_all(stage, v, result, lanes_of)
+            after(v)
+        return carry
+
+    lax.fori_loop(0, 2, some, 0)
 
 
 def device_index():
@@ -166,14 +168,15 @@
 
 
 def early_blocks():
-    return jnp.where((device_index() >> 1) & 3 == 0, 3, 2).astype(jnp.int32)
+    z = (device_index() >> 1) & 3
+    return jnp.where(z == 0, 3, jnp.where(z == 3, 1, 2)).astype(jnp.int32)
 
 
 def block_at(p, leaver):
     return jnp.where(p == 0, leaver, staying(p - 1, leaver))
 
 
-def first_kernel(migration, neighbours, pop, share, raw, mate, leaving, stage, pop_sem, share_sem, mate_sem):
+def first_kernel(migration, neighbours, pop, share, raw, mate, slots, near, leaving, stage, pop_sem, share_sem, mate_sem):
     lanes_of = lane_tables()
     lane, tables = lanes_of
     segment = lane >> 5
@@ -190,6 +193,10 @@
     for p in range(4):
         for cp in load(p):
             cp.start()
+    for b in range(4):
+        slots[b] = migration[b]
+        for k in range(8):
+            near[b, k] = neighbours[b, k]
 
     pair = (device_index() >> 1) << 3
     tag = jnp.zeros((8, 128), F32)
@@ -295,14 +302,12 @@
 
 
 def late_kernel(neighbours, migration, raw, held, mine, got_in, after, out_in, out, streamed, got,
-                stage, fx, rows, tags, table, tag_sem, out_sem, got_sem, row_sem):
+                stage, fx, rows, table, out_sem, got_sem, row_sem):
     del held, got_in, after, out_in
     lanes_of = lane_tables()
     leaver, moving = leaver_of(migration)
     sub = lax.broadcasted_iota(jnp.int32, (8, 128), 0)
     send = functools.partial(column_send, streamed, out, out_sem, leaver)
-    tag_copy = pltpu.make_async_copy(got.at[TAG_AT, pl.ds(0, 1)], tags, tag_sem)
-    tag_copy.start()
     for s, ref in enumerate((mine, got)):
         fx[s] = ref[pl.ds(FX_AT, 10)]
 
@@ -314,10 +319,9 @@
 
         lax.fori_loop(0, FX_AT, keep, 0)
 
-    tag_copy.wait()
     for p in range(4):
         table[migration[block_at(p, leaver)] & 7] = p
-        table[tags[0, 32 * p].astype(jnp.int32) & 7] = 4 + p
+        table[read(got, TAG_AT, 0, p) & 7] = 4 + p
 
     def incoming(b):
         found = {}
@@ -413,29 +417,24 @@
         arrived(v).wait()
 
 
-def select_kernel(migration, mine, got, after, rise, fall, faces, tags, table, places, tag_sem):
+def read(ref, at, row, segment):
+    return ref[at, row, 32 * segment].astype(jnp.int32)
+
+
+def select_kernel(mine, got, after, rise, fall, faces, table, places):
     del after
-    leaver, _ = leaver_of(migration)
     lane = lax.broadcasted_iota(jnp.int32, (8, 128), 1)
     segment = lane >> 5
-    tag_copies = [
-        pltpu.make_async_copy(ref.at[TAG_AT, pl.ds(0, 2)], tags.at[s], tag_sem.at[s]) for s, ref in enumerate((mine, got))
-    ]
-    for cp in tag_copies:
-        cp.start()
     for s, ref in enumerate((mine, got)):
         for high, at in enumerate((FU_AT, FD_AT)):
             faces[s, high] = ref[pl.ds(at, 5)]
-    for cp in tag_copies:
-        cp.wait()
-    for s in range(2):
         for p in range(4):
-            table[tags[s, 0, 32 * p].astype(jnp.int32) & 7] = 4 * s + p
+            table[read(ref, TAG_AT, 0, p) & 7] = 4 * s + p
     own = (device_index() & 1) * 4
     ups, downs = jnp.int32(0), jnp.int32(0)
-    for s in range(2):
+    for s, ref in enumerate((mine, got)):
         for b in range(4):
-            up = tags[s, 1, 32 * b].astype(jnp.int32)
+            up = read(ref, TAG_AT, 1, b)
             slot = (own ^ (4 * s)) + b
             places[jnp.where(up == 1, ups, 4 + downs)] = slot
             ups, downs = ups + up, downs + 1 - up
@@ -459,19 +458,13 @@
 
 
 def last_kernel(neighbours, migration, mine, low, high, got, streamed_in, out_in,
-                out, streamed, fu, fd, columns, tags, table, tag_sem, got_sem, side_sem):
+                out, streamed, fu, fd, columns, table, got_sem, side_sem):
     del streamed_in, out_in
     pair = (device_index() >> 1) << 3
     leaver, _ = leaver_of(migration)
     lane = lax.broadcasted_iota(jnp.int32, (8, 128), 1)
     sub = lax.broadcasted_iota(jnp.int32, (8, 128), 0)
 
-    tag_copies = [
-        pltpu.make_async_copy(ref, tags.at[pl.ds(k, 1)], tag_sem.at[k])
-        for k, ref in enumerate((got.at[TAG_AT, pl.ds(0, 1)], low.at[20, pl.ds(0, 1)], high.at[20, pl.ds(0, 1)]))
-    ]
-    for cp in tag_copies:
-        cp.start()
     for s, ref in enumerate((mine, got)):
         fu[s] = ref[pl.ds(FU_AT, 5)]
         fd[s] = ref[pl.ds(FD_AT, 5)]
@@ -481,12 +474,11 @@
     for high_side in range(2):
         columns[high_side] = got[pl.ds(19 * 7 * high_side, 19)]
 
-    for cp in tag_copies:
-        cp.wait()
     for p in range(4):
         table[migration[block_at(p, leaver)] & 7] = p
-        for k, (start, source) in enumerate(((0, 1), (8, 2), (16, 2))):
-            table[start + (tags[k, 32 * p].astype(jnp.int32) & 7)] = 4 * source + p
+        table[read(got, TAG_AT, 0, p) & 7] = 4 + p
+        table[8 + (read(low, 20, 0, p) & 7)] = 8 + p
+        table[16 + (read(high, 20, 0, p) & 7)] = 8 + p
 
     def find(b, k, beside):
         slot = neighbours[b, k]
@@ -582,12 +574,14 @@
     def cost(flops, data):
         return pl.CostEstimate(flops=flops, bytes_accessed=data, transcendentals=0)
 
-    raw, mate = pl.pallas_call(
+    slots_shape = pltpu.SMEM((4,), jnp.int32)
+    near_shape = pltpu.SMEM((4, 8), jnp.int32)
+    raw, mate, migration, neighbours = pl.pallas_call(
         first_kernel,
         name="faces_and_leaver",
-        out_shape=(pltpu.VMEM((4, 20, 32, 1024), F32), mate_shape),
+        out_shape=(pltpu.VMEM((4, 20, 32, 1024), F32), mate_shape, slots_shape, near_shape),
         in_specs=[SMEM, SMEM, HBM, HBM],
-        out_specs=(VMEM,) * 2,
+        out_specs=(VMEM, VMEM, SMEM, SMEM),
         scratch_shapes=[pltpu.VMEM((19, 10, 48, 128), F32), stage, dma((4,)), dma((4,)), dma((8,))],
         compiler_params=params(8),
         cost_estimate=cost(20_000_000, 12_000_000),
@@ -611,18 +605,16 @@
         select_kernel,
         name="select_faces",
         out_shape=(halo_shape, halo_shape),
-        in_specs=[SMEM, VMEM, VMEM, VMEM],
+        in_specs=[VMEM, VMEM, VMEM],
         out_specs=(VMEM, VMEM),
         scratch_shapes=[
             pltpu.VMEM((2, 2, 5, 32, 128), F32),
-            pltpu.SMEM((2, 2, 128), F32),
             pltpu.SMEM((8,), jnp.int32),
             pltpu.SMEM((8,), jnp.int32),
-            dma((2,)),
         ],
         compiler_params=params(4),
         cost_estimate=cost(1_000_000, 1_000_000),
-    )(migration, mate, got, streamed)
+    )(mate, got, streamed)
     high = lax.ppermute(fall, axes, route(-2, 0))
     low = lax.ppermute(rise, axes, route(2, 0))
 
@@ -637,9 +629,8 @@
             stage,
             pltpu.VMEM((2, 10, 32, 128), F32),
             pltpu.VMEM((3, 2, 14, 8, 768), F32),
-            pltpu.SMEM((1, 128), F32),
             pltpu.SMEM((8,), jnp.int32),
-            dma, dma((3, 8)), dma((8,)), dma((3, 2)),
+            dma((3, 8)), dma((8,)), dma((3, 2)),
         ],
         compiler_params=params(6),
         cost_estimate=cost(30_000_000, 16_000_000),
@@ -656,9 +647,8 @@
             pltpu.VMEM((3, 5, 32, 128), F32),
             pltpu.VMEM((3, 5, 32, 128), F32),
             pltpu.VMEM((2, 19, 32, 128), F32),
-            pltpu.SMEM((3, 128), F32),
             pltpu.SMEM((24,), jnp.int32),
-            dma((3,)), dma((2,)), dma((3, 2)),
+            dma((2,)), dma((3, 2)),
         ],
         compiler_params=params(6),
         cost_estimate=cost(1_000_000, 8_000_000),

time: 29.7 us -> 26.3 us (0.89)
  Pallas kernels: 21 us -> 16.8 us
  waiting for transfers between devices: 0.01 us -> 0.88 us
    pallas_call x1, Pallas kernels: 2.96 us -> 1.76 us  [on_device(): pl.pallas_call(last_kernel, name='outer_columns', out_shape=(out_shape, s...]
    pallas_call x1, Pallas kernels: 1.55 us -> 0.4 us  [on_device(): pl.pallas_call(select_kernel, name='select_faces', out_shape=(halo_shape,...]
    pallas_call x1, Pallas kernels: 2.94 us -> 1.8 us  [on_device(): pl.pallas_call(late_kernel, name='late_blocks', out_shape=(out_shape, str...]
    ppermute x1, waiting for transfers between devices: 0.01 us -> 0.87 us  [on_device(): low = lax.ppermute(rise, axes, route(2, 0))]
    pallas_call x1, Pallas kernels: 7.44 us -> 6.75 us  [on_device(): pl.pallas_call(early_kernel, name='early_blocks', out_shape=(out_shape, s...]
  transfers between devices with their start and end apart: 3 -> 3, of which waited for: 0 -> 1; matrix products, arithmetic and copies ran while one was open for 0% -> 0% of each run, Pallas kernels for 35% -> 33%
where the time goes in v4:
time: 26.3 us; the launch traced here: 26.2 us
  Pallas kernels  16.8 us (64%)
  starting transfers between devices  8.46 us (32%)
  waiting for transfers between devices  0.88 us (3%)
    ppermute x1, starting transfers between devices, on_device(): high = lax.ppermute(fall, axes, route(-2, 0))  6.88 us
    pallas_call x1, Pallas kernels, on_device(): pl.pallas_call(early_kernel, name='early_blocks', out_shape=(out_shape, s...  6.75 us
    pallas_call x1, Pallas kernels, on_device(): pl.pallas_call(first_kernel, name='faces_and_leaver', out_shape=(pltpu.VM...  6.08 us
    pallas_call x1, Pallas kernels, on_device(): pl.pallas_call(late_kernel, name='late_blocks', out_shape=(out_shape, str...  1.8 us
    pallas_call x1, Pallas kernels, on_device(): pl.pallas_call(last_kernel, name='outer_columns', out_shape=(out_shape, s...  1.76 us
    ppermute x1, starting transfers between devices, on_device(): got = lax.ppermute(mate, axes, route(0, 1))  1.5 us
    ppermute x1, waiting for transfers between devices, on_device(): low = lax.ppermute(rise, axes, route(2, 0))  0.87 us
  transfers between devices with their start and end apart: 3, of which 1 were waited for; matrix products, arithmetic and copies ran while one was open for 0% of the time, Pallas kernels for 33%

profile of v4, /device:TPU:1, one launch (start us, length us, event | category | flops | bytes accessed | tf_op | source)
XLA Modules:
  0.0 26.2 jit_solution(9066853084103300721)
XLA Ops:
  0.0 6.1 %faces_and_leaver.1 = (f32[4,20,32,1024]{3,2,1,0:T(8,128)S(1)}, f32[173,32,128]{2,1,0:T(8,128)S(1)}, s32[4]{0:T(128)S(4)}, s32[4,8]{1,0:T(4,128)S(4)}) custom-call(s32[4]{0:T(128)} %migration.1, s32[4,8]{1,0:T(4,128)} %neighbours.1, f32[4,19,32,1024]{3,2,1,0:T(8,128)} %pop.1, f32[4,32,1024]{2,1,0:T(8,128)} %share.1), custom_call_target="tpu_custom_call" | custom-call | flops 20000000 | bytes 12000000 | tf_op jit(solution)/shard_map/faces_and_leaver/pallas_call | solution.py:579
  6.1 1.5 %collective-permute-start = (f32[173,32,128]{2,1,0:T(8,128)S(1)}, f32[173,32,128]{2,1,0:T(8,128)S(1)}, u32[]{:S(2)}, u32[]{:S(2)}) collective-permute-start(f32[173,32,128]{2,1,0:T(8,128)S(1)} %get-tuple-element.19.after.mine), channel_id=1, source_target_pairs={{0,1},{1,0},{2,3},{3,2},{4,5},{5,4},{6,7},{7,6},{8,9},{9,8},{10,11... | collective-permute-start | bytes 8503304 | tf_op jit(solution)/shard_map/ppermute | solution.py:591
  7.6 6.8 %early_blocks.1 = (f32[4,19,32,1024]{3,2,1,0:T(8,128)}, f32[3,19,10,48,128]{4,3,2,1,0:T(8,128)S(1)}) custom-call(s32[4]{0:T(128)S(4)} %get-tuple-element.18.migration, f32[4,20,32,1024]{3,2,1,0:T(8,128)S(1)} %get-tuple-element.20.raw, f32[173,32,128]{2,1,0:T(8,128)S(1)} %get-tuple-element.19.after.mine), custom_call_target="tpu_custom_call" | custom-call | flops 30000000 | bytes 16000000 | tf_op jit(solution)/shard_map/early_blocks/pallas_call | solution.py:593
  14.4 0.0 collective-permute-done.got.got_in
  14.4 0.4 %select_faces.1 = (f32[21,8,128]{2,1,0:T(8,128)S(1)}, f32[21,8,128]{2,1,0:T(8,128)S(1)}) custom-call(f32[173,32,128]{2,1,0:T(8,128)S(1)} %get-tuple-element.19.after.mine, f32[173,32,128]{2,1,0:T(8,128)S(1)} %collective-permute-done.got.got_in, f32[3,19,10,48,128]{4,3,2,1,0:T(8,128)S(1)} %get-tuple-element.21.after.held), custom_call_target="tpu_custom_call" | custom-call | flops 1000000 | bytes 1000000 | tf_op jit(solution)/shard_map/select_faces/pallas_call | solution.py:604
  14.8 0.1 collective-permute-start.1
  14.8 6.9 %collective-permute-start.2 = (f32[21,8,128]{2,1,0:T(8,128)S(1)}, f32[21,8,128]{2,1,0:T(8,128)S(1)}, u32[]{:S(2)}, u32[]{:S(2)}) collective-permute-start(f32[21,8,128]{2,1,0:T(8,128)S(1)} %get-tuple-element.23.after), channel_id=1, source_target_pairs={{0,126},{1,127},{2,0},{3,1},{4,2},{5,3},{6,4},{7,5},{8,6},{9,7},{1... | collective-permute-start | bytes 258056 | tf_op jit(solution)/shard_map/ppermute | solution.py:618
  21.7 1.8 %late_blocks.1 = (f32[4,19,32,1024]{3,2,1,0:T(8,128)}, f32[3,19,10,48,128]{4,3,2,1,0:T(8,128)S(1)}, f32[173,32,128]{2,1,0:T(8,128)S(1)}) custom-call(s32[4,8]{1,0:T(4,128)S(4)} %get-tuple-element.17.neighbours, s32[4]{0:T(128)S(4)} %get-tuple-element.18.migration, ...), custom_call_target="tpu_custom_call", output_to_operand_aliasing={{0}: (7, {}), {1}: (3, {}), {2}: (5, {})} | custom-call | flops 30000000 | bytes 16000000 | tf_op jit(solution)/shard_map/late_blocks/pallas_call | solution.py:621
  23.5 0.9 %collective-permute-done.1.low = f32[21,8,128]{2,1,0:T(8,128)S(1)} collective-permute-done((f32[21,8,128]{2,1,0:T(8,128)S(1)}, f32[21,8,128]{2,1,0:T(8,128)S(1)}, u32[]{:S(2)}, u32[]{:S(2)}) %collective-permute-start.1) | collective-permute-done | bytes 86048 | tf_op jit(solution)/shard_map/ppermute | solution.py:619
  24.4 0.0 collective-permute-done.2.high
  24.4 1.8 %outer_columns.1 = (f32[4,19,32,1024]{3,2,1,0:T(8,128)}, f32[3,19,10,48,128]{4,3,2,1,0:T(8,128)S(1)}) custom-call(s32[4,8]{1,0:T(4,128)S(4)} %get-tuple-element.17.neighbours, s32[4]{0:T(128)S(4)} %get-tuple-element.18.migration, f32[173,32,128]{2,1,0:T(8,128)S(1)} %get-tuple-element.19.after.mine, ...), custom_call_target="tpu_custom_call", output_to_operand_aliasing={{0}: (7, {}), {1}: (6, {})} | custom-call | flops 1000000 | bytes 8000000 | tf_op jit(solution)/shard_map/outer_columns/pallas_call | solution.py:639
Async XLA Ops:
  6.1 8.3 %collective-permute-start = (f32[173,32,128]{2,1,0:T(8,128)S(1)}, f32[173,32,128]{2,1,0:T(8,128)S(1)}, u32[]{:S(2)}, u32[]{:S(2)}) collective-permute-start(f32[173,32,128]{2,1,0:T(8,128)S(1)} %get-tuple-element.19.after.mine), channel_id=1, source_target_pairs={{0,1},{1,0},{2,3},{3,2},{4,5},{5,4},{6,7},{7,6},{8,9},{9,8},{10,11... | collective-permute-start | bytes 8503304 | tf_op jit(solution)/shard_map/ppermute | solution.py:591
  14.8 9.6 %collective-permute-start.1 = (f32[21,8,128]{2,1,0:T(8,128)S(1)}, f32[21,8,128]{2,1,0:T(8,128)S(1)}, u32[]{:S(2)}, u32[]{:S(2)}) collective-permute-start(f32[21,8,128]{2,1,0:T(8,128)S(1)} %get-tuple-element.22), channel_id=1, source_target_pairs={{0,2},{1,3},{2,4},{3,5},{4,6},{5,7},{6,8},{7,9},{8,10},{9,11},{10,... | collective-permute-start | bytes 258056 | tf_op jit(solution)/shard_map/ppermute | solution.py:619
  14.8 9.6 %collective-permute-start.2 = (f32[21,8,128]{2,1,0:T(8,128)S(1)}, f32[21,8,128]{2,1,0:T(8,128)S(1)}, u32[]{:S(2)}, u32[]{:S(2)}) collective-permute-start(f32[21,8,128]{2,1,0:T(8,128)S(1)} %get-tuple-element.23.after), channel_id=1, source_target_pairs={{0,126},{1,127},{2,0},{3,1},{4,2},{5,3},{6,4},{7,5},{8,6},{9,7},{1... | collective-permute-start | bytes 258056 | tf_op jit(solution)/shard_map/ppermute | solution.py:618

commit v5 on v4

--- a/solution.py
+++ b/solution.py
@@ -135,8 +135,9 @@
                 pltpu.store(result.at[c, column + 1 + step_y, to, :], value, mask=out)
 
 
-def process(source, result, stage, lanes_of, after):
+def process(source, result, stage, lanes_of, after, before=lambda i: None):
     def some(i, carry):
+        before(i)
         for h in range(4):
             v = 4 * i + h
             for part in range(4):
@@ -176,7 +177,7 @@
     return jnp.where(p == 0, leaver, staying(p - 1, leaver))
 
 
-def first_kernel(migration, neighbours, pop, share, raw, mate, slots, near, leaving, stage, pop_sem, share_sem, mate_sem):
+def first_kernel(migration, neighbours, pop, share, raw, mate, slots, near, leaving, stage, half_sem, pop_sem, share_sem, mate_sem):
     lanes_of = lane_tables()
     lane, tables = lanes_of
     segment = lane >> 5
@@ -190,7 +191,16 @@
             pltpu.make_async_copy(share.at[b], raw.at[p, 19], share_sem.at[p]),
         )
 
-    for p in range(4):
+    def half(h):
+        lanes = pl.ds(512 * h, 512)
+        return (
+            pltpu.make_async_copy(pop.at[leaver, :, :, lanes], raw.at[0, pl.ds(0, 19), :, lanes], half_sem.at[0, h]),
+            pltpu.make_async_copy(share.at[leaver, :, lanes], raw.at[0, 19, :, lanes], half_sem.at[1, h]),
+        )
+
+    for cp in half(0) + half(1):
+        cp.start()
+    for p in range(1, 4):
         for cp in load(p):
             cp.start()
     for b in range(4):
@@ -218,19 +228,15 @@
             post = collide([ends(c) for c in range(19)], ends(19))
             for comps, at, shift in ((YU, FU_AT, 32 * p + 32), (YD, FD_AT, 32 * p)):
                 for i, c in enumerate(comps):
-                    value = pltpu.roll(turn(post[c], 0, VELOCITY[c][2], tables), shift & 127, 1)
+                    value = turn(post[c], 0, VELOCITY[c][2], tables)
+                    value = pltpu.roll(value, shift % 128, 1) if shift % 128 else value
                     pltpu.store(mate.at[at + i, rows, :], value, mask=mine)
 
         for end, comps in ((0, XP), (1, XM)):
 
             def packed(c):
-                got = None
-                for v in range(8):
-                    x = raw[p, c, pl.ds(24 - 24 * end, 8), pl.ds(128 * v, 128)]
-                    shift = (v + 1 - end) % 8
-                    x = pltpu.roll(x, shift, 0) if shift else x
-                    got = x if got is None else jnp.where(sub == v, x, got)
-                return got
+                row = pl.ds(31 - 31 * end, 1)
+                return jnp.concatenate([raw[p, c, row, pl.ds(128 * v, 128)] for v in range(8)], axis=0)
 
             post = collide([packed(c) for c in range(19)], packed(19))
             for i, c in enumerate(comps):
@@ -239,31 +245,34 @@
                 if step_y:
                     out = (lane < 32) if step_y == 1 else (lane >= 96)
                     value = jnp.where(out, pltpu.roll(value, step_y % 8, 0), value)
-                mate[FX_AT + 5 * end + i, pl.ds(pl.multiple_of(8 * p, 8), 8), :] = value
+                mate[FX_AT + 5 * end + i, pl.ds(8 * p, 8), :] = value
 
     def hand(v):
         return pltpu.make_async_copy(
             leaving.at[:, v + 1, pl.ds(8, 32), :], mate.at[pl.ds(19 * v, 19)], mate_sem.at[v]
         )
 
-    def work(p, carry):
-        for cp in load(p):
-            cp.wait()
-        faces(p)
-
-        @pl.when(p == 0)
+    def before(i):
+        for h in range(2):
+            @pl.when(i == h)
+            def _(h=h):
+                for cp in half(h):
+                    cp.wait()
+
+    def after(v):
+        @pl.when(v > 0)
         def _():
-            def after(v):
-                @pl.when(v > 0)
-                def _():
-                    hand(v - 1).start()
-
-            process(raw.at[0], leaving, stage, lanes_of, after)
-            hand(7).start()
-
-        return carry
-
-    lax.fori_loop(0, 4, work, 0)
+            hand(v - 1).start()
+
+    process(raw.at[0], leaving, stage, lanes_of, after, before)
+    hand(7).start()
+    for group in ((0, 1), (2,), (3,)):
+        for p in group:
+            if p:
+                for cp in load(p):
+                    cp.wait()
+        for p in group:
+            faces(p)
     for v in range(8):
         hand(v).wait()
 
@@ -457,9 +466,9 @@
                 halo[4 * i + part] = got_tile
 
 
-def last_kernel(neighbours, migration, mine, low, high, got, streamed_in, out_in,
-                out, streamed, fu, fd, columns, table, got_sem, side_sem):
-    del streamed_in, out_in
+def last_kernel(neighbours, migration, mine, low, high, got_in, streamed_in, out_in,
+                out, streamed, got, fu, fd, table, got_sem, side_sem):
+    del got_in, streamed_in, out_in
     pair = (device_index() >> 1) << 3
     leaver, _ = leaver_of(migration)
     lane = lax.broadcasted_iota(jnp.int32, (8, 128), 1)
@@ -471,8 +480,6 @@
     for n in range(20):
         fu[2, n // 4, pl.ds(8 * (n % 4), 8), :] = low[n]
         fd[2, n // 4, pl.ds(8 * (n % 4), 8), :] = high[n]
-    for high_side in range(2):
-        columns[high_side] = got[pl.ds(19 * 7 * high_side, 19)]
 
     for p in range(4):
         table[migration[block_at(p, leaver)] & 7] = p
@@ -516,10 +523,10 @@
 
     def send_arrived(upper):
         return pltpu.make_async_copy(
-            columns.at[upper], out.at[leaver, :, :, pl.ds(896 * upper, 128)], got_sem.at[upper]
+            got.at[pl.ds(133 * upper, 19)], out.at[leaver, :, :, pl.ds(896 * upper, 128)], got_sem.at[upper]
         )
 
-    patch_columns(leaver, lambda c, part, upper: columns.at[upper, c, pl.ds(8 * part, 8), :])
+    patch_columns(leaver, lambda c, part, upper: got.at[133 * upper + c, pl.ds(8 * part, 8), :])
     for upper in range(2):
         send_arrived(upper).start()
 
@@ -582,7 +589,7 @@
         out_shape=(pltpu.VMEM((4, 20, 32, 1024), F32), mate_shape, slots_shape, near_shape),
         in_specs=[SMEM, SMEM, HBM, HBM],
         out_specs=(VMEM, VMEM, SMEM, SMEM),
-        scratch_shapes=[pltpu.VMEM((19, 10, 48, 128), F32), stage, dma((4,)), dma((4,)), dma((8,))],
+        scratch_shapes=[pltpu.VMEM((19, 10, 48, 128), F32), stage, dma((2, 2)), dma((4,)), dma((4,)), dma((8,))],
         compiler_params=params(8),
         cost_estimate=cost(20_000_000, 12_000_000),
     )(migration, neighbours, populations, solid_share)
@@ -636,17 +643,16 @@
         cost_estimate=cost(30_000_000, 16_000_000),
     )(neighbours, migration, raw, streamed, mate, got, fall, out)
 
-    out, _ = pl.pallas_call(
+    out, _, _ = pl.pallas_call(
         last_kernel,
         name="outer_columns",
-        out_shape=(out_shape, stream_shape),
+        out_shape=(out_shape, stream_shape, mate_shape),
         in_specs=[SMEM, SMEM] + [VMEM] * 5 + [HBM],
-        out_specs=(HBM, VMEM),
-        input_output_aliases={7: 0, 6: 1},
+        out_specs=(HBM, VMEM, VMEM),
+        input_output_aliases={7: 0, 6: 1, 5: 2},
         scratch_shapes=[
             pltpu.VMEM((3, 5, 32, 128), F32),
             pltpu.VMEM((3, 5, 32, 128), F32),
-            pltpu.VMEM((2, 19, 32, 128), F32),
             pltpu.SMEM((24,), jnp.int32),
             dma((2,)), dma((3, 2)),
         ],

time: 26.3 us -> 25.6 us (0.973)
  Pallas kernels: 16.8 us -> 16.1 us
    pallas_call x1, Pallas kernels: 6.08 us -> 5.44 us  [on_device(): pl.pallas_call(first_kernel, name='faces_and_leaver', out_shape=(pltpu.VM...]
  transfers between devices with their start and end apart: 3 -> 3, of which waited for: 1 -> 1; matrix products, arithmetic and copies ran while one was open for 0% -> 0% of each run, Pallas kernels for 33% -> 34%
where the time goes in v5:
time: 25.6 us; the launch traced here: 25.5 us
  Pallas kernels  16.1 us (63%)
  starting transfers between devices  8.46 us (33%)
  waiting for transfers between devices  0.88 us (3%)
    ppermute x1, starting transfers between devices, on_device(): high = lax.ppermute(fall, axes, route(-2, 0))  6.88 us
    pallas_call x1, Pallas kernels, on_device(): pl.pallas_call(early_kernel, name='early_blocks', out_shape=(out_shape, s...  6.75 us
    pallas_call x1, Pallas kernels, on_device(): pl.pallas_call(first_kernel, name='faces_and_leaver', out_shape=(pltpu.VM...  5.44 us
    pallas_call x1, Pallas kernels, on_device(): pl.pallas_call(late_kernel, name='late_blocks', out_shape=(out_shape, str...  1.8 us
    pallas_call x1, Pallas kernels, on_device(): pl.pallas_call(last_kernel, name='outer_columns', out_shape=(out_shape, s...  1.75 us
    ppermute x1, starting transfers between devices, on_device(): got = lax.ppermute(mate, axes, route(0, 1))  1.5 us
    ppermute x1, waiting for transfers between devices, on_device(): low = lax.ppermute(rise, axes, route(2, 0))  0.88 us
  transfers between devices with their start and end apart: 3, of which 1 were waited for; matrix products, arithmetic and copies ran while one was open for 0% of the time, Pallas kernels for 34%

profile of v5, /device:TPU:1, one launch (start us, length us, event | category | flops | bytes accessed | tf_op | source)
XLA Modules:
  0.0 25.5 jit_solution(7798839151335794861)
XLA Ops:
  0.0 5.4 %faces_and_leaver.1 = (f32[4,20,32,1024]{3,2,1,0:T(8,128)S(1)}, f32[173,32,128]{2,1,0:T(8,128)S(1)}, s32[4]{0:T(128)S(4)}, s32[4,8]{1,0:T(4,128)S(4)}) custom-call(s32[4]{0:T(128)} %migration.1, s32[4,8]{1,0:T(4,128)} %neighbours.1, f32[4,19,32,1024]{3,2,1,0:T(8,128)} %pop.1, f32[4,32,1024]{2,1,0:T(8,128)} %share.1), custom_call_target="tpu_custom_call" | custom-call | flops 20000000 | bytes 12000000 | tf_op jit(solution)/shard_map/faces_and_leaver/pallas_call | solution.py:586
  5.4 1.5 %collective-permute-start = (f32[173,32,128]{2,1,0:T(8,128)S(1)}, f32[173,32,128]{2,1,0:T(8,128)S(1)}, u32[]{:S(2)}, u32[]{:S(2)}) collective-permute-start(f32[173,32,128]{2,1,0:T(8,128)S(1)} %get-tuple-element.19.after.mine), channel_id=1, source_target_pairs={{0,1},{1,0},{2,3},{3,2},{4,5},{5,4},{6,7},{7,6},{8,9},{9,8},{10,11... | collective-permute-start | bytes 8503304 | tf_op jit(solution)/shard_map/ppermute | solution.py:598
  6.9 6.8 %early_blocks.1 = (f32[4,19,32,1024]{3,2,1,0:T(8,128)}, f32[3,19,10,48,128]{4,3,2,1,0:T(8,128)S(1)}) custom-call(s32[4]{0:T(128)S(4)} %get-tuple-element.18.migration, f32[4,20,32,1024]{3,2,1,0:T(8,128)S(1)} %get-tuple-element.20.raw, f32[173,32,128]{2,1,0:T(8,128)S(1)} %get-tuple-element.19.after.mine), custom_call_target="tpu_custom_call" | custom-call | flops 30000000 | bytes 16000000 | tf_op jit(solution)/shard_map/early_blocks/pallas_call | solution.py:600
  13.7 0.0 collective-permute-done.got.got_in
  13.7 0.4 %select_faces.1 = (f32[21,8,128]{2,1,0:T(8,128)S(1)}, f32[21,8,128]{2,1,0:T(8,128)S(1)}) custom-call(f32[173,32,128]{2,1,0:T(8,128)S(1)} %get-tuple-element.19.after.mine, f32[173,32,128]{2,1,0:T(8,128)S(1)} %collective-permute-done.got.got_in, f32[3,19,10,48,128]{4,3,2,1,0:T(8,128)S(1)} %get-tuple-element.21.after.held), custom_call_target="tpu_custom_call" | custom-call | flops 1000000 | bytes 1000000 | tf_op jit(solution)/shard_map/select_faces/pallas_call | solution.py:611
  14.1 0.1 collective-permute-start.1
  14.2 6.9 %collective-permute-start.2 = (f32[21,8,128]{2,1,0:T(8,128)S(1)}, f32[21,8,128]{2,1,0:T(8,128)S(1)}, u32[]{:S(2)}, u32[]{:S(2)}) collective-permute-start(f32[21,8,128]{2,1,0:T(8,128)S(1)} %get-tuple-element.23.after), channel_id=1, source_target_pairs={{0,126},{1,127},{2,0},{3,1},{4,2},{5,3},{6,4},{7,5},{8,6},{9,7},{1... | collective-permute-start | bytes 258056 | tf_op jit(solution)/shard_map/ppermute | solution.py:625
  21.1 1.8 %late_blocks.1 = (f32[4,19,32,1024]{3,2,1,0:T(8,128)}, f32[3,19,10,48,128]{4,3,2,1,0:T(8,128)S(1)}, f32[173,32,128]{2,1,0:T(8,128)S(1)}) custom-call(s32[4,8]{1,0:T(4,128)S(4)} %get-tuple-element.17.neighbours, s32[4]{0:T(128)S(4)} %get-tuple-element.18.migration, ...), custom_call_target="tpu_custom_call", output_to_operand_aliasing={{0}: (7, {}), {1}: (3, {}), {2}: (5, {})} | custom-call | flops 30000000 | bytes 16000000 | tf_op jit(solution)/shard_map/late_blocks/pallas_call | solution.py:628
  22.9 0.9 %collective-permute-done.1.low = f32[21,8,128]{2,1,0:T(8,128)S(1)} collective-permute-done((f32[21,8,128]{2,1,0:T(8,128)S(1)}, f32[21,8,128]{2,1,0:T(8,128)S(1)}, u32[]{:S(2)}, u32[]{:S(2)}) %collective-permute-start.1) | collective-permute-done | bytes 86048 | tf_op jit(solution)/shard_map/ppermute | solution.py:626
  23.8 0.0 collective-permute-done.2.high
  23.8 1.8 %outer_columns.1 = (f32[4,19,32,1024]{3,2,1,0:T(8,128)}, f32[3,19,10,48,128]{4,3,2,1,0:T(8,128)S(1)}, f32[173,32,128]{2,1,0:T(8,128)S(1)}) custom-call(s32[4,8]{1,0:T(4,128)S(4)} %get-tuple-element.17.neighbours, s32[4]{0:T(128)S(4)} %get-tuple-element.18.migration, ...), custom_call_target="tpu_custom_call", output_to_operand_aliasing={{0}: (7, {}), {1}: (6, {}), {2}: (5, {})} | custom-call | flops 1000000 | bytes 8000000 | tf_op jit(solution)/shard_map/outer_columns/pallas_call | solution.py:646
Async XLA Ops:
  5.4 8.3 %collective-permute-start = (f32[173,32,128]{2,1,0:T(8,128)S(1)}, f32[173,32,128]{2,1,0:T(8,128)S(1)}, u32[]{:S(2)}, u32[]{:S(2)}) collective-permute-start(f32[173,32,128]{2,1,0:T(8,128)S(1)} %get-tuple-element.19.after.mine), channel_id=1, source_target_pairs={{0,1},{1,0},{2,3},{3,2},{4,5},{5,4},{6,7},{7,6},{8,9},{9,8},{10,11... | collective-permute-start | bytes 8503304 | tf_op jit(solution)/shard_map/ppermute | solution.py:598
  14.1 9.6 %collective-permute-start.1 = (f32[21,8,128]{2,1,0:T(8,128)S(1)}, f32[21,8,128]{2,1,0:T(8,128)S(1)}, u32[]{:S(2)}, u32[]{:S(2)}) collective-permute-start(f32[21,8,128]{2,1,0:T(8,128)S(1)} %get-tuple-element.22), channel_id=1, source_target_pairs={{0,2},{1,3},{2,4},{3,5},{4,6},{5,7},{6,8},{7,9},{8,10},{9,11},{10,... | collective-permute-start | bytes 258056 | tf_op jit(solution)/shard_map/ppermute | solution.py:626
  14.2 9.6 %collective-permute-start.2 = (f32[21,8,128]{2,1,0:T(8,128)S(1)}, f32[21,8,128]{2,1,0:T(8,128)S(1)}, u32[]{:S(2)}, u32[]{:S(2)}) collective-permute-start(f32[21,8,128]{2,1,0:T(8,128)S(1)} %get-tuple-element.23.after), channel_id=1, source_target_pairs={{0,126},{1,127},{2,0},{3,1},{4,2},{5,3},{6,4},{7,5},{8,6},{9,7},{1... | collective-permute-start | bytes 258056 | tf_op jit(solution)/shard_map/ppermute | solution.py:625

commit v6 on v5

--- a/solution.py
+++ b/solution.py
@@ -311,7 +311,7 @@
 
 
 def late_kernel(neighbours, migration, raw, held, mine, got_in, after, out_in, out, streamed, got,
-                stage, fx, rows, table, out_sem, got_sem, row_sem):
+                stage, fx, rows, table, out_sem, got_sem, row_sem, still_sem):
     del held, got_in, after, out_in
     lanes_of = lane_tables()
     leaver, moving = leaver_of(migration)
@@ -361,10 +361,18 @@
             got.at[pl.ds(19 * v, 19)], out.at[leaver, :, :, pl.ds(128 * v, 128)], got_sem.at[v]
         )
 
+    def still(p, upper):
+        few, at = pl.ds(0, 3), pl.ds(896 * upper, 128)
+        source = got.at[pl.ds(133 * upper, 3)] if p is None else streamed.at[p - 1, few, 1 + 7 * upper, pl.ds(8, 32), :]
+        b = leaver if p is None else block_at(p, leaver)
+        return pltpu.make_async_copy(source, out.at[b, few, :, at], still_sem.at[0 if p is None else p, upper])
+
     for v in range(8):
         patch_column(xs, v, lambda c, row: got.at[19 * v + c, pl.ds(row, 8), :])
         if 0 < v < 7:
             arrived(v).start()
+        else:
+            still(None, v // 7).start()
 
     def send_rows(p):
         return [
@@ -389,6 +397,7 @@
             cp.start()
         for v in (0, 7):
             patch_column(xs, v, streamed_at(p, v))
+            still(p, v // 7).start()
         return carry
 
     def remaining(p, carry):
@@ -405,6 +414,8 @@
 
         process(raw.at[p], streamed.at[p - 1], stage, lanes_of, after_column)
         patch_column(xs, 7, streamed_at(p, 7))
+        for upper in range(2):
+            still(p, upper).start()
         return carry
 
     def finish(p, carry):
@@ -424,6 +435,10 @@
     lax.fori_loop(middle, 4, finish, 0)
     for v in range(1, 7):
         arrived(v).wait()
+    for upper in range(2):
+        still(None, upper).wait()
+        for p in range(1, 4):
+            still(p, upper).wait()
 
 
 def read(ref, at, row, segment):
@@ -523,7 +538,9 @@
 
     def send_arrived(upper):
         return pltpu.make_async_copy(
-            got.at[pl.ds(133 * upper, 19)], out.at[leaver, :, :, pl.ds(896 * upper, 128)], got_sem.at[upper]
+            got.at[pl.ds(133 * upper + 3, 16)],
+            out.at[leaver, pl.ds(3, 16), :, pl.ds(896 * upper, 128)],
+            got_sem.at[upper],
         )
 
     patch_columns(leaver, lambda c, part, upper: got.at[133 * upper + c, pl.ds(8 * part, 8), :])
@@ -533,8 +550,8 @@
     def send_sides(p):
         return [
             pltpu.make_async_copy(
-                streamed.at[p - 1, :, 1 + 7 * upper, pl.ds(8, 32), :],
-                out.at[block_at(p, leaver), :, :, pl.ds(896 * upper, 128)],
+                streamed.at[p - 1, pl.ds(3, 16), 1 + 7 * upper, pl.ds(8, 32), :],
+                out.at[block_at(p, leaver), pl.ds(3, 16), :, pl.ds(896 * upper, 128)],
                 side_sem.at[p - 1, upper],
             )
             for upper in range(2)
@@ -637,7 +654,7 @@
             pltpu.VMEM((2, 10, 32, 128), F32),
             pltpu.VMEM((3, 2, 14, 8, 768), F32),
             pltpu.SMEM((8,), jnp.int32),
-            dma((3, 8)), dma((8,)), dma((3, 2)),
+            dma((3, 8)), dma((8,)), dma((3, 2)), dma((4, 2)),
         ],
         compiler_params=params(6),
         cost_estimate=cost(30_000_000, 16_000_000),

time: 25.6 us -> 25.5 us (level)
  no operation moved by 1% of the time
where the time goes in v6:
time: 25.5 us; the launch traced here: 25.4 us
  Pallas kernels  16.2 us (64%)
  starting transfers between devices  8.46 us (33%)
  waiting for transfers between devices  0.69 us (3%)
    ppermute x1, starting transfers between devices, on_device(): high = lax.ppermute(fall, axes, route(-2, 0))  6.88 us
    pallas_call x1, Pallas kernels, on_device(): pl.pallas_call(early_kernel, name='early_blocks', out_shape=(out_shape, s...  6.75 us
    pallas_call x1, Pallas kernels, on_device(): pl.pallas_call(first_kernel, name='faces_and_leaver', out_shape=(pltpu.VM...  5.44 us
    pallas_call x1, Pallas kernels, on_device(): pl.pallas_call(late_kernel, name='late_blocks', out_shape=(out_shape, str...  1.98 us
    pallas_call x1, Pallas kernels, on_device(): pl.pallas_call(last_kernel, name='outer_columns', out_shape=(out_shape, s...  1.62 us
    ppermute x1, starting transfers between devices, on_device(): got = lax.ppermute(mate, axes, route(0, 1))  1.5 us
    ppermute x1, waiting for transfers between devices, on_device(): low = lax.ppermute(rise, axes, route(2, 0))  0.69 us
  transfers between devices with their start and end apart: 3, of which 1 were waited for; matrix products, arithmetic and copies ran while one was open for 0% of the time, Pallas kernels for 34%

profile of v6, /device:TPU:1, one launch (start us, length us, event | category | flops | bytes accessed | tf_op | source)
XLA Modules:
  0.0 25.4 jit_solution(3796338288342583208)
XLA Ops:
  0.0 5.4 %faces_and_leaver.1 = (f32[4,20,32,1024]{3,2,1,0:T(8,128)S(1)}, f32[173,32,128]{2,1,0:T(8,128)S(1)}, s32[4]{0:T(128)S(4)}, s32[4,8]{1,0:T(4,128)S(4)}) custom-call(s32[4]{0:T(128)} %migration.1, s32[4,8]{1,0:T(4,128)} %neighbours.1, f32[4,19,32,1024]{3,2,1,0:T(8,128)} %pop.1, f32[4,32,1024]{2,1,0:T(8,128)} %share.1), custom_call_target="tpu_custom_call" | custom-call | flops 20000000 | bytes 12000000 | tf_op jit(solution)/shard_map/faces_and_leaver/pallas_call | solution.py:603
  5.4 1.5 %collective-permute-start = (f32[173,32,128]{2,1,0:T(8,128)S(1)}, f32[173,32,128]{2,1,0:T(8,128)S(1)}, u32[]{:S(2)}, u32[]{:S(2)}) collective-permute-start(f32[173,32,128]{2,1,0:T(8,128)S(1)} %get-tuple-element.19.after.mine), channel_id=1, source_target_pairs={{0,1},{1,0},{2,3},{3,2},{4,5},{5,4},{6,7},{7,6},{8,9},{9,8},{10,11... | collective-permute-start | bytes 8503304 | tf_op jit(solution)/shard_map/ppermute | solution.py:615
  6.9 6.8 %early_blocks.1 = (f32[4,19,32,1024]{3,2,1,0:T(8,128)}, f32[3,19,10,48,128]{4,3,2,1,0:T(8,128)S(1)}) custom-call(s32[4]{0:T(128)S(4)} %get-tuple-element.18.migration, f32[4,20,32,1024]{3,2,1,0:T(8,128)S(1)} %get-tuple-element.20.raw, f32[173,32,128]{2,1,0:T(8,128)S(1)} %get-tuple-element.19.after.mine), custom_call_target="tpu_custom_call" | custom-call | flops 30000000 | bytes 16000000 | tf_op jit(solution)/shard_map/early_blocks/pallas_call | solution.py:617
  13.7 0.0 collective-permute-done.got.got_in
  13.7 0.4 %select_faces.1 = (f32[21,8,128]{2,1,0:T(8,128)S(1)}, f32[21,8,128]{2,1,0:T(8,128)S(1)}) custom-call(f32[173,32,128]{2,1,0:T(8,128)S(1)} %get-tuple-element.19.after.mine, f32[173,32,128]{2,1,0:T(8,128)S(1)} %collective-permute-done.got.got_in, f32[3,19,10,48,128]{4,3,2,1,0:T(8,128)S(1)} %get-tuple-element.21.after.held), custom_call_target="tpu_custom_call" | custom-call | flops 1000000 | bytes 1000000 | tf_op jit(solution)/shard_map/select_faces/pallas_call | solution.py:628
  14.1 0.1 collective-permute-start.1
  14.2 6.9 %collective-permute-start.2 = (f32[21,8,128]{2,1,0:T(8,128)S(1)}, f32[21,8,128]{2,1,0:T(8,128)S(1)}, u32[]{:S(2)}, u32[]{:S(2)}) collective-permute-start(f32[21,8,128]{2,1,0:T(8,128)S(1)} %get-tuple-element.23.after), channel_id=1, source_target_pairs={{0,126},{1,127},{2,0},{3,1},{4,2},{5,3},{6,4},{7,5},{8,6},{9,7},{1... | collective-permute-start | bytes 258056 | tf_op jit(solution)/shard_map/ppermute | solution.py:642
  21.1 2.0 %late_blocks.1 = (f32[4,19,32,1024]{3,2,1,0:T(8,128)}, f32[3,19,10,48,128]{4,3,2,1,0:T(8,128)S(1)}, f32[173,32,128]{2,1,0:T(8,128)S(1)}) custom-call(s32[4,8]{1,0:T(4,128)S(4)} %get-tuple-element.17.neighbours, s32[4]{0:T(128)S(4)} %get-tuple-element.18.migration, ...), custom_call_target="tpu_custom_call", output_to_operand_aliasing={{0}: (7, {}), {1}: (3, {}), {2}: (5, {})} | custom-call | flops 30000000 | bytes 16000000 | tf_op jit(solution)/shard_map/late_blocks/pallas_call | solution.py:645
  23.1 0.7 %collective-permute-done.1.low = f32[21,8,128]{2,1,0:T(8,128)S(1)} collective-permute-done((f32[21,8,128]{2,1,0:T(8,128)S(1)}, f32[21,8,128]{2,1,0:T(8,128)S(1)}, u32[]{:S(2)}, u32[]{:S(2)}) %collective-permute-start.1) | collective-permute-done | bytes 86048 | tf_op jit(solution)/shard_map/ppermute | solution.py:643
  23.8 0.0 collective-permute-done.2.high
  23.8 1.6 %outer_columns.1 = (f32[4,19,32,1024]{3,2,1,0:T(8,128)}, f32[3,19,10,48,128]{4,3,2,1,0:T(8,128)S(1)}, f32[173,32,128]{2,1,0:T(8,128)S(1)}) custom-call(s32[4,8]{1,0:T(4,128)S(4)} %get-tuple-element.17.neighbours, s32[4]{0:T(128)S(4)} %get-tuple-element.18.migration, ...), custom_call_target="tpu_custom_call", output_to_operand_aliasing={{0}: (7, {}), {1}: (6, {}), {2}: (5, {})} | custom-call | flops 1000000 | bytes 8000000 | tf_op jit(solution)/shard_map/outer_columns/pallas_call | solution.py:663
Async XLA Ops:
  5.4 8.3 %collective-permute-start = (f32[173,32,128]{2,1,0:T(8,128)S(1)}, f32[173,32,128]{2,1,0:T(8,128)S(1)}, u32[]{:S(2)}, u32[]{:S(2)}) collective-permute-start(f32[173,32,128]{2,1,0:T(8,128)S(1)} %get-tuple-element.19.after.mine), channel_id=1, source_target_pairs={{0,1},{1,0},{2,3},{3,2},{4,5},{5,4},{6,7},{7,6},{8,9},{9,8},{10,11... | collective-permute-start | bytes 8503304 | tf_op jit(solution)/shard_map/ppermute | solution.py:615
  14.1 9.6 %collective-permute-start.1 = (f32[21,8,128]{2,1,0:T(8,128)S(1)}, f32[21,8,128]{2,1,0:T(8,128)S(1)}, u32[]{:S(2)}, u32[]{:S(2)}) collective-permute-start(f32[21,8,128]{2,1,0:T(8,128)S(1)} %get-tuple-element.22), channel_id=1, source_target_pairs={{0,2},{1,3},{2,4},{3,5},{4,6},{5,7},{6,8},{7,9},{8,10},{9,11},{10,... | collective-permute-start | bytes 258056 | tf_op jit(solution)/shard_map/ppermute | solution.py:643
  14.2 9.6 %collective-permute-start.2 = (f32[21,8,128]{2,1,0:T(8,128)S(1)}, f32[21,8,128]{2,1,0:T(8,128)S(1)}, u32[]{:S(2)}, u32[]{:S(2)}) collective-permute-start(f32[21,8,128]{2,1,0:T(8,128)S(1)} %get-tuple-element.23.after), channel_id=1, source_target_pairs={{0,126},{1,127},{2,0},{3,1},{4,2},{5,3},{6,4},{7,5},{8,6},{9,7},{1... | collective-permute-start | bytes 258056 | tf_op jit(solution)/shard_map/ppermute | solution.py:642
